TPU v7x, 512 devices: a whole 4x4x16 slice. The times are simulated.
512 devices in a mesh: dp: 2 (over x_lo), segment: 16 (over x_hi, y, core), space: 16 (over z).
Axes of the slice: x: 4 (x_hi: 2, x_lo: 2; x = x_hi * 2 + x_lo), y: 4, z: 16, core: 2. Of those that a mesh axis runs over, the one named last changes fastest.
Arguments:
- features: bfloat16 [2, 16, 32, 96, 6, 256], P('dp', 'segment', None, 'space'), may hold values from -6 to 6
- out_grad: bfloat16 [2, 16, 64, 48, 3, 128], P('dp', 'segment', None, 'space'), may hold values from -6 to 6
- weight_mean: float32 [16, 27, 2048], P('segment'), may hold values from -0.21875 to 0.21875
- weight_noise: float32 [16, 27, 2048], P('segment'), may hold values from -4 to 4
- precision: float32 [16, 27, 2048], P('segment'), may hold values from 0.5 to 4
Outputs:
- act_in: bfloat16 [2, 16, 64, 48, 3, 128], P('dp', 'segment', None, 'space')
- grad_in: bfloat16 [2, 16, 32, 96, 6, 256], P('dp', 'segment', None, 'space')
- mean_next: float32 [16, 27, 2048], P('segment')
- precision_next: float32 [16, 27, 2048], P('segment')
All inputs are finite; a program needn't handle non-finite values.
Results may differ from a plain program's by a relative error of at most 0.007.
Values may be sent and summed in bfloat16 or wider, within the bound.
A program may use at most 64 MiB of HBM per device.

v0:
```python
import math

import jax
import jax.numpy as jnp
from jax import lax
from jax.sharding import PartitionSpec as P

CONV_LAYOUT = ("NCDHW", "OIDHW", "NCDHW")


def passed_along(block, axis, distance):
    devices = range(lax.axis_size(axis))
    route = [(i - distance, i) for i in devices if i - distance in devices]
    return lax.ppermute(block, axis, route)


def split_up(shard, dim, length):
    before, after = (shard.shape[:dim], shard.shape[dim + 1 :])
    return jnp.moveaxis(shard.reshape(*before, length, -1, *after), dim, 0)


def sum_at_owner(shard, axis, dim):
    blocks = split_up(shard, dim, lax.axis_size(axis))
    arrived = lax.all_to_all(blocks, axis, split_axis=0, concat_axis=0, tiled=True)
    return arrived.astype(jnp.float32).sum(axis=0)


def in_order(blocks, dim):
    dims = list(blocks.shape[1:])
    dims[dim] *= blocks.shape[0]
    return jnp.moveaxis(blocks, 0, dim).reshape(dims)


def copy_for_each(shard, axis):
    length = lax.axis_size(axis)
    return lax.all_to_all(
        jnp.broadcast_to(shard[None], (length, *shard.shape)), axis, 0, 0, tiled=True
    )


def gather_directly(shard, axis, dim):
    return in_order(copy_for_each(shard, axis), dim)


def noisy_weights(weight_mean, weight_noise, precision, cout, cin):
    noisy = weight_mean + weight_noise * lax.rsqrt(2000.0 * (precision + 0.1))
    kernel = noisy.astype(jnp.bfloat16).reshape(3, 3, 3, cout, cin)
    return jnp.transpose(kernel, (3, 4, 0, 1, 2))


def forward_conv(padded, kernel):
    return lax.conv_general_dilated(
        padded[None],
        kernel,
        (2, 2, 2),
        "VALID",
        dimension_numbers=CONV_LAYOUT,
        preferred_element_type=jnp.float32,
    )[0]


def input_conv(pre_grad, kernel):
    flipped = jnp.transpose(kernel[:, :, ::-1, ::-1, ::-1], (1, 0, 2, 3, 4))
    return lax.conv_general_dilated(
        pre_grad[None],
        flipped,
        (1, 1, 1),
        ((2, 2), (2, 2), (2, 2)),
        lhs_dilation=(2, 2, 2),
        dimension_numbers=CONV_LAYOUT,
        preferred_element_type=jnp.float32,
    )[0]


def weight_conv(padded, pre_grad):
    grads = lax.conv_general_dilated(
        padded[:, None],
        pre_grad[:, None],
        (1, 1, 1),
        "VALID",
        rhs_dilation=(2, 2, 2),
        dimension_numbers=CONV_LAYOUT,
        preferred_element_type=jnp.float32,
    )
    return jnp.transpose(grads, (2, 3, 4, 1, 0)).reshape(27, -1)


def input_grad(pre_grad, kernel):
    spread_grad = input_conv(pre_grad, kernel)
    rim_plane = passed_along(spread_grad[:, 0, 1:, 1:], "space", -1)
    interior = spread_grad[:, 1:, 1:, 1:]
    interior = jnp.concatenate([interior[:, :-1], interior[:, -1:] + rim_plane[:, None]], axis=1)
    return interior.astype(jnp.bfloat16)


def per_device(features, out_grad, weight_mean, weight_noise, precision):
    feats = features[0, 0]
    grads = out_grad[0, 0]
    mean = weight_mean[0]
    prec = precision[0]
    cin = feats.shape[0]
    cout = grads.shape[0]
    kernel = noisy_weights(mean, weight_noise[0], prec, cout, cin)
    below = passed_along(feats[:, -1:], "space", 1)
    padded = jnp.pad(jnp.concatenate([below, feats], axis=1), ((0, 0), (0, 0), (1, 0), (1, 0)))
    preact = forward_conv(padded, kernel)
    activation = jax.nn.silu(preact).astype(jnp.bfloat16)
    act_in = passed_along(activation, "segment", 1)
    squash = jax.nn.sigmoid(preact)
    pre_grad = (grads.astype(jnp.float32) * squash * (1.0 + preact * (1.0 - squash))).astype(
        jnp.bfloat16
    )
    grad_in = passed_along(input_grad(pre_grad, kernel), "segment", -1)
    local_grad = weight_conv(padded, pre_grad)
    cell_count = (
        lax.axis_size("dp")
        * lax.axis_size("space")
        * pre_grad.shape[1]
        * pre_grad.shape[2]
        * pre_grad.shape[3]
    )
    inv_root = 1.0 / math.sqrt(cell_count)
    grad_part = sum_at_owner(local_grad.astype(jnp.bfloat16), ("dp", "space"), 1)
    share_width = grad_part.shape[1]
    offset = lax.axis_index(("dp", "space")) * share_width
    prec_part = lax.dynamic_slice_in_dim(prec, offset, share_width, 1)
    mean_part = lax.dynamic_slice_in_dim(mean, offset, share_width, 1)
    scaled = grad_part * inv_root
    prec_piece = 0.75 * prec_part + 0.25 * scaled * scaled
    mean_piece = mean_part - 0.03 * scaled / (prec_piece + 0.1)
    mean_new, prec_next = (
        gather_directly(mean_piece, ("dp", "space"), 1),
        gather_directly(prec_piece, ("dp", "space"), 1),
    )
    return (act_in[None, None], grad_in[None, None], mean_new[None], prec_next[None])


def solution(mesh):
    in_specs = (
        P("dp", "segment", None, "space", None, None),
        P("dp", "segment", None, "space", None, None),
        P("segment", None, None),
        P("segment", None, None),
        P("segment", None, None),
    )
    out_specs = (
        P("dp", "segment", None, "space", None, None),
        P("dp", "segment", None, "space", None, None),
        P("segment", None, None),
        P("segment", None, None),
    )
    return jax.shard_map(
        per_device, mesh=mesh, in_specs=in_specs, out_specs=out_specs, check_vma=False
    )
```

profile of v0, /device:TPU:24, one launch (start us, length us, event | category | flops | bytes accessed | tf_op | source)
XLA Modules:
  0.0 158.3 jit_solution(13922880213419366699)
XLA Ops:
  0.6 0.9 slice.26
  1.5 3.8 %collective-permute-start = (bf16[32,1,6,256]{3,0,2,1:T(8,128)(2,1)S(1)}, bf16[32,1,6,256]{3,0,2,1:T(8,128)(2,1)S(1)}, u32[]{:S(2)}, u32[]{:S(2)}) collective-permute-start(bf16[32,1,6,256]{3,0,2,1:T(8,128)(2,1)S(1)} %slice.26), channel_id=1, source_target_pairs={{0,1},{1,2},{2,3},{3,4},{4,5},{5,6},{6,7},{7,8},{8,9},{9,10},{10,1... | collective-permute-start | bytes 294920 | tf_op jit(solution)/shard_map/ppermute | solution.py:14
  5.4 2.0 %convert_reduce_fusion.1 = bf16[27,2048]{1,0:T(8,128)(2,1)S(1)} fusion(f32[1,27,2048]{2,0,1:T(1,128)} %param.7, f32[1,27,2048]{2,0,1:T(1,128)} %param.8, f32[1,27,2048]{2,0,1:T(1,128)} %param.9), kind=kLoop, calls=%fused_computation.53 | loop fusion | flops 276480 | bytes 774144 | tf_op jit(solution)/shard_map/convert_element_type | solution.py:47
  7.4 1.1 reshape.150
  8.4 2.6 %fusion.49 = (bf16[32,1,7,7,257]{4,0,3,2,1:T(8,128)(2,1)}, bf16[32,7,7,1,257]{4,0,2,1,3:T(8,128)(2,1)S(1)}) fusion(bf16[32,6,6,256]{3,0,2,1:T(8,128)(2,1)} %bitcast.115, bf16[32,1,6,256]{3,0,2,1:T(8,128)(2,1)S(1)} %collective-permute-done), kind=kLoop, calls=%fused_computation.72 | loop fusion | flops 4432736 | bytes 2300032 | tf_op jit(solution)/shard_map/broadcast_in_dim | solution.py:77
  11.0 1.2 pad.5
  12.2 4.4 %reshape.120 = bf16[32,7,7,1,8,34]{5,4,0,2,1,3:T(8,128)(2,1)S(1)} reshape(bf16[32,7,7,1,272]{4,0,2,1,3:T(8,128)(2,1)} %pad.5) | data formatting | bytes 1705984 | tf_op jit(solution)/shard_map/conv_general_dilated | solution.py:52
  16.6 5.3 %copy.61 = bf16[32,7,7,1,8,34]{0,4,5,2,1,3:T(8,128)(2,1)} copy(bf16[32,7,7,1,8,34]{5,4,0,2,1,3:T(8,128)(2,1)S(1)} %reshape.120) | data formatting | bytes 1705984 | tf_op jit(solution)/shard_map/conv_general_dilated | solution.py:52
  21.9 1.0 slice.27
  22.9 5.1 %add_divide_fusion = (f32[3,3,8,17,64]{4,2,3,1,0:T(8,128)}, f32[3,3,8,17,64]{4,2,3,1,0:T(8,128)S(1)}, f32[3,3,8,17,64]{4,2,3,1,0:T(8,128)S(1)}) fusion(bf16[3,3,3,64,32]{4,3,2,1,0:T(8,128)(2,1)} %reshape.150, bf16[32,7,7,1,7,2]{0,4,5,2,1,3:T(8,128)(2,1)S(1)} %slice.27, bf16[32,7,7,1,8,34]{0,4,5,2,1,3:T(8,128)(2,1)} %copy.61, pred[8,17]{0,1:T(8,128)(4,1)S(1)} %copy-done.6), kind=kOutput, calls=%fused_computation.25 | convolution fusion | flops 138622464 | bytes 1947656 | tf_op jit(solution)/shard_map/conv_general_dilated | solution.py:52
  28.0 0.1 copy.62
  28.3 0.2 copy.83
  28.5 0.4 copy-done.4
  28.9 0.1 fusion.30
  29.0 0.6 copy.73
  29.6 13.4 %copy.72 = bf16[32,1,7,7,257]{0,1,4,3,2:T(2,128)(2,1)} copy(bf16[32,1,7,7,257]{4,0,3,2,1:T(8,128)(2,1)S(1)} %copy-done) | data formatting | bytes 1611904 | tf_op jit(solution)/shard_map/broadcast_in_dim | solution.py:77
  43.0 15.2 %convolution_convert_fusion = bf16[3,3,3,64,32]{3,4,2,1,0:T(8,128)(2,1)S(1)} fusion(bf16[32,1,7,7,257]{0,1,4,3,2:T(2,128)(2,1)} %copy.72, bf16[64,1,3,3,128]{0,1,4,3,2:T(2,128)(2,1)S(1)} %copy.73), kind=kOutput, calls=%fused_computation.19 | convolution fusion | flops 127457280 | bytes 1064000 | tf_op jit(solution)/shard_map/transpose | solution.py:85
  58.2 0.3 copy.74
  58.5 0.2 convert_element_type.67
  58.7 0.1 copy.75
  58.8 0.9 reshape.152
  59.7 17.4 %all-to-all-start = ((bf16[32,2,864]{2,1,0:T(2,128)(2,1)}), bf16[32,2,864]{2,1,0:T(2,128)(2,1)S(1)}, u32[]{:S(2)}, u32[]{:S(2)}) async-start(bf16[32,2,864]{2,1,0:T(2,128)(2,1)} %reshape.152), calls=%async_computation | async-start | bytes 229376 | tf_op jit(solution)/shard_map/all_to_all | solution.py:24
  77.1 0.1 copy.64
  77.3 0.2 copy.84
  77.5 0.1 copy.66
  77.8 0.2 copy.85
  78.0 0.1 fusion.41
  78.1 0.2 copy.86
  78.3 0.1 pad.7.clone
  78.5 0.1 reshape.127
  78.6 13.4 %all-to-all-done = bf16[32,2,864]{2,1,0:T(2,128)(2,1)S(1)} async-done(((bf16[32,2,864]{2,1,0:T(2,128)(2,1)}), bf16[32,2,864]{2,1,0:T(2,128)(2,1)S(1)}, u32[]{:S(2)}, u32[]{:S(2)}) %all-to-all-start) | async-done | bytes 110624 | tf_op jit(solution)/shard_map/all_to_all | solution.py:24
  92.0 0.2 reshape.153
  92.3 0.1 convert_reduce_fusion
  92.4 0.9 divide_subtract_fusion
  93.3 1.0 reshape.156
  94.3 3.9 %all-to-all-start.2 = ((f32[32,1,1728]{2,1,0:T(1,128)}), f32[32,1,1728]{2,1,0:T(1,128)S(1)}, u32[]{:S(2)}, u32[]{:S(2)}) async-start(f32[32,1,1728]{2,1,0:T(1,128)} %reshape.156), calls=%async_computation.2 | async-start | bytes 458752 | tf_op jit(solution)/shard_map/all_to_all | solution.py:36
  98.2 6.5 %broadcast_select_fusion = f32[7,7,8,34,32]{4,2,3,1,0:T(8,128)} fusion(pred[8,34]{0,1:T(8,128)(4,1)S(1)} %copy-done.5, bf16[3,3,3,64,32]{4,3,2,1,0:T(8,128)(2,1)S(1)} %copy-done.2, bf16[64,3,3,1,7,1]{0,4,5,2,1,3:T(8,128)(2,1)S(1)} %slice.31, bf16[64,3,3,1,8,17]{0,4,5,2,1,3:T(8,128)(2,1)S(1)} %copy.70), kind=kOutput, calls=%fused_computation.8 | convolution fusion | flops 136288768 | bytes 1981584 | tf_op jit(solution)/shard_map/conv_general_dilated | solution.py:64
  104.7 9.6 %copy.71 = f32[7,7,8,34,32]{3,2,4,1,0:T(8,128)} copy(f32[7,7,8,34,32]{4,2,3,1,0:T(8,128)} %broadcast_select_fusion) | data formatting | bytes 3411968 | tf_op jit(solution)/shard_map/conv_general_dilated | solution.py:64
  114.3 4.9 %reshape.131 = f32[7,7,1,272,32]{3,4,1,0,2:T(8,128)S(1)} reshape(f32[7,7,8,34,32]{3,2,4,1,0:T(8,128)} %copy.71) | data formatting | bytes 3411968 | tf_op jit(solution)/shard_map/conv_general_dilated | solution.py:64
  119.1 0.2 slice_bitcast_fusion
  119.3 0.1 slice_bitcast_fusion.1
  119.4 1.3 collective-permute-start.2
  120.7 0.2 slice.42
  121.0 1.0 reshape.154
  122.0 14.3 %all-to-all-start.1 = ((f32[32,1,1728]{2,1,0:T(1,128)}), f32[32,1,1728]{2,1,0:T(1,128)S(1)}, u32[]{:S(2)}, u32[]{:S(2)}) async-start(f32[32,1,1728]{2,1,0:T(1,128)} %reshape.154), calls=%async_computation.1 | async-start | bytes 458752 | tf_op jit(solution)/shard_map/all_to_all | solution.py:36
  136.4 1.1 fusion.39
  137.4 0.1 pad_maximum_fusion
  137.5 1.9 %collective-permute-start.3 = (bf16[32,6,6,256]{3,0,2,1:T(8,128)(2,1)S(1)}, bf16[32,6,6,256]{3,0,2,1:T(8,128)(2,1)S(1)}, u32[]{:S(2)}, u32[]{:S(2)}) collective-permute-start(bf16[32,6,6,256]{3,0,2,1:T(8,128)(2,1)S(1)} %pad_maximum_fusion), channel_id=1, source_target_pairs={{16,0},{32,16},{48,32},{64,48},{80,64},{96,80},{112,96},{128,112},... | collective-permute-start | bytes 1769480 | tf_op jit(solution)/shard_map/ppermute | solution.py:14
  139.4 0.1 fusion.38
  139.5 2.4 %collective-permute-start.1 = (bf16[64,3,3,128]{3,0,2,1:T(8,128)(2,1)S(1)}, bf16[64,3,3,128]{3,0,2,1:T(8,128)(2,1)S(1)}, u32[]{:S(2)}, u32[]{:S(2)}) collective-permute-start(bf16[64,3,3,128]{3,0,2,1:T(8,128)(2,1)S(1)} %fusion.38), channel_id=1, source_target_pairs={{0,16},{16,32},{32,48},{48,64},{64,80},{80,96},{96,112},{112,128},... | collective-permute-start | bytes 442376 | tf_op jit(solution)/shard_map/ppermute | solution.py:14
  141.9 4.0 %collective-permute-done.1 = bf16[64,3,3,128]{3,0,2,1:T(8,128)(2,1)S(1)} collective-permute-done((bf16[64,3,3,128]{3,0,2,1:T(8,128)(2,1)S(1)}, bf16[64,3,3,128]{3,0,2,1:T(8,128)(2,1)S(1)}, u32[]{:S(2)}, u32[]{:S(2)}) %collective-permute-start.1) | collective-permute-done | bytes 147488 | tf_op jit(solution)/shard_map/ppermute | solution.py:14
  146.0 0.8 collective-permute-done.3
  146.8 0.5 broadcast.137
  147.3 1.2 reduce.3
  148.5 0.2 reshape.157
  148.7 0.3 copy.78
  149.0 0.9 broadcast_in_dim_reshape.9
  149.9 4.3 %all-to-all-done.1 = f32[32,1,1728]{2,1,0:T(1,128)S(1)} async-done(((f32[32,1,1728]{2,1,0:T(1,128)}), f32[32,1,1728]{2,1,0:T(1,128)S(1)}, u32[]{:S(2)}, u32[]{:S(2)}) %all-to-all-start.1) | async-done | bytes 221216 | tf_op jit(solution)/shard_map/all_to_all | solution.py:36
  154.2 1.2 reduce.2
  155.4 0.2 reshape.155
  155.6 0.3 copy.77
  155.9 0.9 broadcast_in_dim_reshape.8
  156.8 0.7 copy.93
  157.5 0.8 copy.94
  (28 shorter events, 0.5 us)
Async XLA Ops:
  1.5 6.9 %collective-permute-start = (bf16[32,1,6,256]{3,0,2,1:T(8,128)(2,1)S(1)}, bf16[32,1,6,256]{3,0,2,1:T(8,128)(2,1)S(1)}, u32[]{:S(2)}, u32[]{:S(2)}) collective-permute-start(bf16[32,1,6,256]{3,0,2,1:T(8,128)(2,1)S(1)} %slice.26), channel_id=1, source_target_pairs={{0,1},{1,2},{2,3},{3,4},{4,5},{5,6},{6,7},{7,8},{8,9},{9,10},{10,1... | collective-permute-start | bytes 294920 | tf_op jit(solution)/shard_map/ppermute | solution.py:14
  16.6 6.3 %copy-start.6 = (pred[8,17]{0,1:T(8,128)(4,1)S(1)}, pred[8,17]{0,1:T(8,128)(4,1)}, u32[]{:S(2)}) copy-start(pred[8,17]{0,1:T(8,128)(4,1)} %constant.58) | copy-start | bytes 412
  28.0 0.9 copy-start.4
  28.1 1.5 copy-start
  58.2 18.9 %copy-start.3 = (f32[3,3,8,17,64]{4,2,3,1,0:T(8,128)S(1)}, f32[3,3,8,17,64]{4,2,3,1,0:T(8,128)}, u32[]{:S(2)}) copy-start(f32[3,3,8,17,64]{4,2,3,1,0:T(8,128)} %get-tuple-element.24) | copy-start | bytes 940036
  59.7 32.4 %all-to-all-start = ((bf16[32,2,864]{2,1,0:T(2,128)(2,1)}), bf16[32,2,864]{2,1,0:T(2,128)(2,1)S(1)}, u32[]{:S(2)}, u32[]{:S(2)}) async-start(bf16[32,2,864]{2,1,0:T(2,128)(2,1)} %reshape.152), calls=%async_computation | async-start | bytes 229376 | tf_op jit(solution)/shard_map/all_to_all | solution.py:24
  78.3 19.9 %copy-start.2 = (bf16[3,3,3,64,32]{4,3,2,1,0:T(8,128)(2,1)S(1)}, bf16[3,3,3,64,32]{4,3,2,1,0:T(8,128)(2,1)}, u32[]{:S(2)}) copy-start(bf16[3,3,3,64,32]{4,3,2,1,0:T(8,128)(2,1)} %reshape.150) | copy-start | bytes 331780
  78.3 19.9 %copy-start.5 = (pred[8,34]{0,1:T(8,128)(4,1)S(1)}, pred[8,34]{0,1:T(8,128)(4,1)}, u32[]{:S(2)}) copy-start(pred[8,34]{0,1:T(8,128)(4,1)} %constant.59) | copy-start | bytes 820
  94.3 27.7 %all-to-all-start.2 = ((f32[32,1,1728]{2,1,0:T(1,128)}), f32[32,1,1728]{2,1,0:T(1,128)S(1)}, u32[]{:S(2)}, u32[]{:S(2)}) async-start(f32[32,1,1728]{2,1,0:T(1,128)} %reshape.156), calls=%async_computation.2 | async-start | bytes 458752 | tf_op jit(solution)/shard_map/all_to_all | solution.py:36
  119.3 1.4 copy-start.1
  119.4 16.9 %collective-permute-start.2 = (f32[32,6,256]{2,0,1:T(8,128)S(1)}, f32[32,6,256]{2,0,1:T(8,128)S(1)}, u32[]{:S(2)}, u32[]{:S(2)}) collective-permute-start(f32[32,6,256]{2,0,1:T(8,128)S(1)} %slice_bitcast_fusion.1), channel_id=1, source_target_pairs={{1,0},{2,1},{3,2},{4,3},{5,4},{6,5},{7,6},{8,7},{9,8},{10,9},{11,1... | collective-permute-start | bytes 589832 | tf_op jit(solution)/shard_map/ppermute | solution.py:14
  122.0 32.2 %all-to-all-start.1 = ((f32[32,1,1728]{2,1,0:T(1,128)}), f32[32,1,1728]{2,1,0:T(1,128)S(1)}, u32[]{:S(2)}, u32[]{:S(2)}) async-start(f32[32,1,1728]{2,1,0:T(1,128)} %reshape.154), calls=%async_computation.1 | async-start | bytes 458752 | tf_op jit(solution)/shard_map/all_to_all | solution.py:36
  137.5 9.3 %collective-permute-start.3 = (bf16[32,6,6,256]{3,0,2,1:T(8,128)(2,1)S(1)}, bf16[32,6,6,256]{3,0,2,1:T(8,128)(2,1)S(1)}, u32[]{:S(2)}, u32[]{:S(2)}) collective-permute-start(bf16[32,6,6,256]{3,0,2,1:T(8,128)(2,1)S(1)} %pad_maximum_fusion), channel_id=1, source_target_pairs={{16,0},{32,16},{48,32},{64,48},{80,64},{96,80},{112,96},{128,112},... | collective-permute-start | bytes 1769480 | tf_op jit(solution)/shard_map/ppermute | solution.py:14
  139.5 6.5 %collective-permute-start.1 = (bf16[64,3,3,128]{3,0,2,1:T(8,128)(2,1)S(1)}, bf16[64,3,3,128]{3,0,2,1:T(8,128)(2,1)S(1)}, u32[]{:S(2)}, u32[]{:S(2)}) collective-permute-start(bf16[64,3,3,128]{3,0,2,1:T(8,128)(2,1)S(1)} %fusion.38), channel_id=1, source_target_pairs={{0,16},{16,32},{32,48},{48,64},{64,80},{80,96},{96,112},{112,128},... | collective-permute-start | bytes 442376 | tf_op jit(solution)/shard_map/ppermute | solution.py:14
where the time goes:
time: 159 us; the launch traced here: 158 us
  local copies, waits for them, and re-layouts  53.5 us (34%)
  starting transfers between devices  45 us (28%)
  matrix products  26.8 us (17%)
  waiting for transfers between devices  22.6 us (14%)
  other arithmetic  9.3 us (6%)
    all_to_all x2, starting transfers between devices, copy_for_each(): lax.all_to_all(jnp.broadcast_to(shard[None], (length, *shard.shape)), axi...  18.2 us
    all_to_all x1, starting transfers between devices, sum_at_owner(): lax.all_to_all(blocks, axis, split_axis=0, concat_axis=0, tiled=True)  17.4 us
    transpose x1, matrix products, weight_conv(): return jnp.transpose(grads, (2, 3, 4, 1, 0)).reshape(27, -1)  15.2 us
    conv_general_dilated x5, local copies, waits for them, and re-layouts, input_conv(): lax.conv_general_dilated(pre_grad[None], flipped, (1, 1, 1), ((2, 2), (2,...  14.6 us
    all_to_all x1, waiting for transfers between devices, sum_at_owner(): lax.all_to_all(blocks, axis, split_axis=0, concat_axis=0, tiled=True)  13.4 us
    broadcast_in_dim x1, local copies, waits for them, and re-layouts, weight_conv(): padded[:, None]  13.4 us
    conv_general_dilated x6, local copies, waits for them, and re-layouts, forward_conv(): lax.conv_general_dilated(padded[None], kernel, (2, 2, 2), 'VALID', dimens...  10.9 us
    ppermute x4, starting transfers between devices, passed_along(): return lax.ppermute(block, axis, route)  9.43 us
  transfers between devices with their start and end apart: 7, of which 4 were waited for; matrix products, arithmetic and copies ran while one was open for 20% of the time, Pallas kernels for 0%

commit v1 on v0

v1 whole, which is shorter than its diff:
```python
import functools
import math

import jax
import jax.numpy as jnp
from jax import lax
from jax.experimental import pallas as pl
from jax.experimental.pallas import tpu as pltpu
from jax.sharding import PartitionSpec as P

MESH = pl.DeviceIdType.MESH
BF16, F32 = jnp.bfloat16, jnp.float32
TAPS = 27
GROUPS = 7


def matmul(a, b, contract=((1,), (0,))):
    return lax.dot_general(a, b, (contract, ((), ())), preferred_element_type=F32)


def kernel(
    n_dp, n_seg, n_space, per_owner,
    feats, og, mean, noise, prec,
    act_out, gin_out, mean_out, prec_out,
    cells, wts, wtr, l_own, l_got, halo, act_own, act_got, pg_own, pg_got, shifted,
    grads, tiles, rs_got, total, ag_got,
    p_send, p_recv, rs_send, rs_recv, ag_send, ag_recv,
):
    dp, seg, space = (lax.axis_index(a) for a in ("dp", "segment", "space"))
    n_group = n_dp * n_space
    owners = -(-TAPS // per_owner)
    me = dp * n_space + space
    first_seg, last_seg = seg == 0, seg == n_seg - 1
    has_next, has_prev = seg < n_seg - 1, seg > 0
    has_up, has_down = space < n_space - 1, space > 0

    def at(d, s, z):
        return {"dp": d, "segment": s, "space": z}

    def peer(k):
        other = lax.rem(me + k, n_group)
        return other, at(other // n_space, seg, lax.rem(other, n_space))

    barrier = pltpu.get_barrier_semaphore()

    def greet(k, carry):
        pl.semaphore_signal(barrier, inc=1, device_id=peer(k)[1], device_id_type=MESH)
        return carry

    lax.fori_loop(1, n_group, greet, 0)
    for cond, to in (
        (has_prev, at(dp, seg - 1, space)),
        (has_next, at(dp, seg + 1, space)),
        (has_prev & has_down, at(dp, seg - 1, space - 1)),
        (has_next & has_up, at(dp, seg + 1, space + 1)),
    ):
        @pl.when(cond)
        def _():
            pl.semaphore_signal(barrier, inc=1, device_id=to, device_id_type=MESH)

    def link(i, src, dst, to):
        return pltpu.make_async_remote_copy(
            src_ref=src, dst_ref=dst, send_sem=p_send.at[i], recv_sem=p_recv.at[i],
            device_id=to, device_id_type=MESH,
        )

    prev = at(dp, seg - 1, space)
    after = at(dp, seg + 1, space)
    links = [
        (link(0, feats.at[feats.shape[0] - 1], halo, at(dp, seg, space + 1)), has_up, has_down),
        (link(1, l_own, l_got, prev), has_prev, has_next),
        (link(2, act_own.at[pl.ds(1, 2)], act_got.at[pl.ds(1, 2)], after), has_next, has_prev),
        (link(3, act_own.at[0], act_got.at[0], after), has_next, has_prev),
        (link(4, pg_own.at[pl.ds(1, 2)], pg_got.at[pl.ds(1, 2)], prev), has_prev, has_next),
        (link(5, pg_own.at[0], pg_got.at[0], prev), has_prev, has_next),
        (
            link(6, pg_own.at[0], pg_got.at[3], at(dp, seg - 1, space - 1)),
            has_prev & has_down,
            has_next & has_up,
        ),
    ]

    def start(i):
        copy, sends, _ = links[i]

        @pl.when(sends)
        def _():
            copy.start()

    def arrived(i):
        copy, _, receives = links[i]

        @pl.when(receives)
        def _():
            copy.wait_recv()

    def sent(i):
        copy, sends, _ = links[i]

        @pl.when(sends)
        def _():
            copy.wait_send()

    lane = lax.broadcasted_iota(jnp.int32, (16, 128), 1)
    chunk = lane // 32

    slabs = []
    for t in range(TAPS):
        rows = pl.ds(16 * t, 16)
        slabs.append(mean[rows] + noise[rows] * lax.rsqrt(2000.0 * (prec[rows] + 0.1)))
    for g in range(GROUPS):
        for low in range(4):
            block = jnp.zeros((16, 128), F32)
            for tl in range(4):
                if 4 * g + tl < TAPS:
                    turned = slabs[4 * g + tl]
                    if tl != low:
                        turned = pltpu.roll(turned, ((tl - low) * 32) % 128, 1)
                    block = jnp.where(chunk == tl, turned, block)
            wts[g, pl.ds(low, 16, stride=4), :] = block

    peers = (
        n_group - 1
        + has_prev.astype(jnp.int32)
        + has_next.astype(jnp.int32)
        + (has_prev & has_down).astype(jnp.int32)
        + (has_next & has_up).astype(jnp.int32)
    )
    pl.semaphore_wait(barrier, peers)
    start(0)

    z_of = lax.broadcasted_iota(jnp.int32, (256, 384), 0)
    column = lax.broadcasted_iota(jnp.int32, (256, 384), 1)
    pick = (z_of == 2 * (column % 128) + column // 128 - 1).astype(F32).astype(BF16)

    def spread(plane, x):
        got = matmul(plane.reshape(192, 256), pick).astype(BF16)
        for y in range(6):
            for e in range(3):
                cells[x, y + 1, pl.ds(32 * e, 32), :] = got[
                    32 * y : 32 * y + 32, 128 * e : 128 * e + 128
                ]

    for x in range(7):
        cells[x, 0] = jnp.zeros((96, 128), BF16)

    def patch(i):
        blocks = []
        for j in range(3):
            parts = [cells[2 * i + a, 2 * j : 2 * j + 3].reshape(288, 128) for a in range(3)]
            blocks.append(jnp.concatenate([*parts, jnp.zeros((32, 128), BF16)], axis=0))
        return jnp.concatenate(blocks, axis=1)

    def forward(i, weights):
        preact = matmul(weights, patch(i))
        grad = jnp.concatenate([og[i, j] for j in range(3)], axis=1).astype(F32)
        gate = jax.nn.sigmoid(preact)
        act = (preact * gate).astype(BF16)
        pre_grad = (grad * gate * (1.0 + preact * (1.0 - gate))).astype(BF16)
        for j in range(3):
            act_own[i, j] = act[:, 128 * j : 128 * j + 128]
            pg_own[i, j] = pre_grad[:, 128 * j : 128 * j + 128]

    def flat_weights():
        return jnp.concatenate([wts[g] for g in range(GROUPS)], axis=1).astype(BF16)

    for x in range(6):
        spread(feats[x], x + 1)
    for i in (1, 2):
        forward(i, flat_weights())
    start(2)
    start(4)

    for g in range(GROUPS):
        wtr[pl.ds(128 * g, 128), :] = jnp.concatenate([wts[g], wts[g]], axis=0).T
    half = lax.broadcasted_iota(jnp.int32, (32, 128), 1) < 64
    for ab in range(9):
        w0, w1, w2 = (wtr[pl.ds(32 * (3 * ab + e), 32), :] for e in range(3))
        even = jnp.where(half, w1, 0.0)
        odd = jnp.where(half, w2, w0)
        l_own[ab] = jnp.concatenate([even, odd], axis=0).astype(BF16)
    start(1)

    @pl.when(has_down)
    def _():
        arrived(0)
        spread(halo[...], 0)

    @pl.when(jnp.logical_not(has_down))
    def _():
        cells[0] = jnp.zeros(cells.shape[1:], BF16)

    forward(0, flat_weights())
    for i in (3, 5, 6):
        start(i)

    for i in (1, 2, 0):
        pre_grad = jnp.concatenate([pg_own[i, j] for j in range(3)], axis=1)
        part = matmul(pre_grad, patch(i), ((1,), (1,)))
        for g in range(GROUPS):
            piece = part[:, 128 * g : 128 * g + 128]
            grads[g] = piece if i == 1 else grads[g] + piece
    for g in range(GROUPS):
        rows = [grads[g, pl.ds(low, 16, stride=4), :] for low in range(4)]
        for tl in range(4):
            t = 4 * g + tl
            if t < TAPS:
                tile = jnp.zeros((16, 128), F32)
                for low in range(4):
                    turned = rows[low]
                    if tl != low:
                        turned = pltpu.roll(turned, ((low - tl) * 32) % 128, 1)
                    tile = jnp.where(chunk == low, turned, tile)
                tiles[t] = tile.astype(BF16)
    for t in range(TAPS, tiles.shape[0]):
        tiles[t] = jnp.zeros((16, 128), BF16)

    def rs_copy(other, to):
        return pltpu.make_async_remote_copy(
            src_ref=tiles.at[pl.ds(other * per_owner, per_owner)], dst_ref=rs_got.at[me],
            send_sem=rs_send.at[other], recv_sem=rs_recv.at[me],
            device_id=to, device_id_type=MESH,
        )

    def rs_arrival(other):
        return pltpu.make_async_remote_copy(
            src_ref=tiles.at[pl.ds(0, per_owner)], dst_ref=rs_got.at[other],
            send_sem=rs_send.at[other], recv_sem=rs_recv.at[other],
            device_id=at(dp, seg, space), device_id_type=MESH,
        )

    def rs_go(k, carry):
        other, to = peer(k)

        @pl.when(other < owners)
        def _():
            rs_copy(other, to).start()

        return carry

    lax.fori_loop(1, n_group, rs_go, 0)

    for i in (2, 3):
        arrived(i)

    @pl.when(has_prev)
    def _():
        act_out[...] = act_got[...]

    @pl.when(first_seg)
    def _():
        act_out[...] = jnp.zeros(act_out.shape, BF16)

    def planes(which, l_rows):
        put_r = lax.broadcasted_iota(jnp.int32, (256, 256), 0)
        put_c = lax.broadcasted_iota(jnp.int32, (256, 256), 1)
        weave = (put_c == 2 * (put_r % 128) + put_r // 128).astype(F32).astype(BF16)
        for i, pp in which:
            rows_i = [(1, i)] if pp == 0 else [(2, i), (0, i + 1)]
            lines = [None] * 6
            for qq in range(2):
                cols_j = [(1, 0)] if qq == 0 else [(2, 0), (0, 1)]
                left = jnp.concatenate(
                    [l_rows[3 * a + b] for a, _ in rows_i for b, _ in cols_j], axis=1
                )
                right = jnp.concatenate(
                    [
                        jnp.concatenate(
                            [shifted[ii, j + dj] for _, ii in rows_i for _, dj in cols_j], axis=0
                        )
                        for j in range(3)
                    ],
                    axis=1,
                )
                got = matmul(left, right).astype(BF16)
                for j in range(3):
                    line = got[:, 128 * j : 128 * j + 128]
                    lines[2 * j + qq] = jnp.concatenate([line[:32], line[32:]], axis=1)
            plane = matmul(jnp.concatenate(lines, axis=0), weave).astype(BF16)
            gin_out[2 * i + pp] = plane.reshape(6, 32, 256)

    inside = lax.broadcasted_iota(jnp.int32, (64, 128), 1) < 127

    def shift(i):
        for j in range(3):
            here = pg_got[i, j]
            moved = jnp.where(inside, pltpu.roll(here.astype(F32), 127, 1), 0.0)
            shifted[i, j, pl.ds(0, 64), :] = here
            shifted[i, j, pl.ds(64, 64), :] = moved.astype(BF16)
        shifted[i, 3] = jnp.zeros((128, 128), BF16)

    arrived(1)
    arrived(4)
    arrived(5)
    arrived(6)

    @pl.when(has_next)
    def _():
        @pl.when(jnp.logical_not(has_up))
        def _():
            pg_got[3] = jnp.zeros(pg_got.shape[1:], BF16)

        for i in range(4):
            shift(i)
        planes([(0, 0), (0, 1), (1, 0), (1, 1), (2, 0), (2, 1)], l_got)

    @pl.when(last_seg)
    def _():
        gin_out[...] = jnp.zeros(gin_out.shape, BF16)

    def ag_copy(other, to):
        return pltpu.make_async_remote_copy(
            src_ref=total, dst_ref=ag_got.at[pl.ds(me * per_owner, per_owner)],
            send_sem=ag_send.at[other], recv_sem=ag_recv.at[me],
            device_id=to, device_id_type=MESH,
        )

    def ag_arrival(other):
        return pltpu.make_async_remote_copy(
            src_ref=total, dst_ref=ag_got.at[pl.ds(other * per_owner, per_owner)],
            send_sem=ag_send.at[other], recv_sem=ag_recv.at[other],
            device_id=at(dp, seg, space), device_id_type=MESH,
        )

    inv_root = 1.0 / math.sqrt(n_group * 3 * 3 * 128)

    @pl.when(me < owners)
    def _():
        rs_got[me] = tiles[pl.ds(me * per_owner, per_owner)]

        def rs_wait(k, carry):
            rs_arrival(peer(k)[0]).wait_recv()
            return carry

        lax.fori_loop(1, n_group, rs_wait, 0)
        summed = rs_got[0].astype(F32)
        for k in range(1, n_group):
            summed += rs_got[k].astype(F32)
        total[...] = (summed * inv_root).astype(BF16)

        def ag_go(k, carry):
            other, to = peer(k)
            ag_copy(other, to).start()
            return carry

        lax.fori_loop(1, n_group, ag_go, 0)
        ag_got[pl.ds(me * per_owner, per_owner)] = total[...]

    def ag_wait(k, carry):
        other, _ = peer(k)

        @pl.when(other < owners)
        def _():
            ag_arrival(other).wait_recv()

        return carry

    lax.fori_loop(1, n_group, ag_wait, 0)
    for t in range(TAPS):
        rows = pl.ds(16 * t, 16)
        scaled = ag_got[t].astype(F32)
        prec_new = 0.75 * prec[rows] + 0.25 * scaled * scaled
        prec_out[rows] = prec_new
        mean_out[rows] = mean[rows] - 0.03 * scaled / (prec_new + 0.1)

    for i in range(len(links)):
        sent(i)

    def rs_sent(k, carry):
        other, to = peer(k)

        @pl.when(other < owners)
        def _():
            rs_copy(other, to).wait_send()

        @pl.when(me < owners)
        def _():
            ag_copy(other, to).wait_send()

        return carry

    lax.fori_loop(1, n_group, rs_sent, 0)


def per_device(features, out_grad, weight_mean, weight_noise, precision):
    n_dp, n_seg, n_space = (lax.axis_size(a) for a in ("dp", "segment", "space"))
    n_group = n_dp * n_space
    per_owner = -(-TAPS // n_group)
    feats = jnp.transpose(features[0, 0], (1, 2, 0, 3))
    og = jnp.transpose(out_grad[0, 0], (1, 2, 0, 3))
    mean, noise, prec = (
        w.reshape(TAPS * 16, 128) for w in (weight_mean, weight_noise, precision)
    )
    vmem = pl.BlockSpec(memory_space=pltpu.VMEM)
    act, gin, mean_new, prec_new = pl.pallas_call(
        functools.partial(kernel, n_dp, n_seg, n_space, per_owner),
        out_shape=[
            jax.ShapeDtypeStruct((3, 3, 64, 128), BF16),
            jax.ShapeDtypeStruct((6, 6, 32, 256), BF16),
            jax.ShapeDtypeStruct((TAPS * 16, 128), F32),
            jax.ShapeDtypeStruct((TAPS * 16, 128), F32),
        ],
        in_specs=[vmem] * 5,
        out_specs=[vmem] * 4,
        scratch_shapes=[
            pltpu.VMEM((7, 7, 96, 128), BF16),
            pltpu.VMEM((GROUPS, 64, 128), F32),
            pltpu.VMEM((GROUPS * 128, 128), F32),
            pltpu.VMEM((9, 64, 128), BF16),
            pltpu.VMEM((9, 64, 128), BF16),
            pltpu.VMEM((6, 32, 256), BF16),
            pltpu.VMEM((3, 3, 64, 128), BF16),
            pltpu.VMEM((3, 3, 64, 128), BF16),
            pltpu.VMEM((3, 3, 64, 128), BF16),
            pltpu.VMEM((4, 3, 64, 128), BF16),
            pltpu.VMEM((4, 4, 128, 128), BF16),
            pltpu.VMEM((GROUPS, 64, 128), F32),
            pltpu.VMEM((n_group * per_owner, 16, 128), BF16),
            pltpu.VMEM((n_group, per_owner, 16, 128), BF16),
            pltpu.VMEM((per_owner, 16, 128), BF16),
            pltpu.VMEM((n_group * per_owner, 16, 128), BF16),
            pltpu.SemaphoreType.DMA((7,)),
            pltpu.SemaphoreType.DMA((7,)),
            pltpu.SemaphoreType.DMA((n_group,)),
            pltpu.SemaphoreType.DMA((n_group,)),
            pltpu.SemaphoreType.DMA((n_group,)),
            pltpu.SemaphoreType.DMA((n_group,)),
        ],
        compiler_params=pltpu.CompilerParams(
            collective_id=0, has_side_effects=True, vmem_limit_bytes=40 * 2**20
        ),
        cost_estimate=pl.CostEstimate(
            flops=600_000_000, bytes_accessed=3_000_000, transcendentals=200_000
        ),
    )(feats, og, mean, noise, prec)
    act = jnp.transpose(act, (2, 0, 1, 3))
    gin = jnp.transpose(gin, (2, 0, 1, 3))
    return (
        act[None, None],
        gin[None, None],
        mean_new.reshape(1, TAPS, 2048),
        prec_new.reshape(1, TAPS, 2048),
    )


def solution(mesh):
    in_specs = (
        P("dp", "segment", None, "space", None, None),
        P("dp", "segment", None, "space", None, None),
        P("segment", None, None),
        P("segment", None, None),
        P("segment", None, None),
    )
    out_specs = (
        P("dp", "segment", None, "space", None, None),
        P("dp", "segment", None, "space", None, None),
        P("segment", None, None),
        P("segment", None, None),
    )
    return jax.shard_map(
        per_device, mesh=mesh, in_specs=in_specs, out_specs=out_specs, check_vma=False
    )
```

time: 159 us -> 49.7 us (0.31)
  local copies, waits for them, and re-layouts: 53.5 us -> 7.62 us
  starting transfers between devices: 45 us -> 0 us
  Pallas kernels: 0 us -> 41.1 us
  matrix products: 26.8 us -> 0 us
  waiting for transfers between devices: 22.6 us -> 0 us
  other arithmetic: 9.3 us -> 0 us
    pallas_call x0 -> x1, Pallas kernels: none -> 41.1 us  [per_device(): pl.pallas_call(functools.partial(kernel, n_dp, n_seg, n_space, per_owner)...]
    all_to_all x3 -> x0, starting transfers between devices: 35.6 us -> none  [the longest x2 18.2 us: copy_for_each(): lax.all_to_all(jnp.broadcast_to(shard[None], (length, *shard.shape)), axi...]
    conv_general_dilated x11 -> x0, local copies, waits for them, and re-layouts: 25.5 us -> none  [the longest x5 14.6 us: input_conv(): lax.conv_general_dilated(pre_grad[None], flipped, (1, 1, 1), ((2, 2), (2,...]
    all_to_all x3 -> x0, waiting for transfers between devices: 17.7 us -> none  [the longest x1 13.4 us: sum_at_owner(): lax.all_to_all(blocks, axis, split_axis=0, concat_axis=0, tiled=True)]
    transpose x1 -> x0, matrix products: 15.2 us -> none  [weight_conv(): return jnp.transpose(grads, (2, 3, 4, 1, 0)).reshape(27, -1)]
    broadcast_in_dim x4 -> x0, local copies, waits for them, and re-layouts: 14.6 us -> none  [the longest x1 13.4 us: weight_conv(): padded[:, None]]
    conv_general_dilated x2 -> x0, matrix products: 11.6 us -> none  [the longest x1 6.48 us: input_conv(): lax.conv_general_dilated(pre_grad[None], flipped, (1, 1, 1), ((2, 2), (2,...]
    ppermute x4 -> x0, starting transfers between devices: 9.43 us -> none  [passed_along(): return lax.ppermute(block, axis, route)]
  transfers between devices with their start and end apart: 7 -> 0, of which waited for: 4 -> 0; matrix products, arithmetic and copies ran while one was open for 20% -> 0% of each run, Pallas kernels for 0% -> 0%
where the time goes in v1:
time: 49.7 us; the launch traced here: 49.4 us
  Pallas kernels  41.1 us (83%)
  local copies, waits for them, and re-layouts  7.62 us (15%)
  between operations  0.65 us (1%)
    pallas_call x1, Pallas kernels, per_device(): pl.pallas_call(functools.partial(kernel, n_dp, n_seg, n_space, per_owner)...  41.1 us
    unnamed x14, local copies, waits for them, and re-layouts  7.62 us

profile of v1, /device:TPU:24, one launch (start us, length us, event | category | flops | bytes accessed | tf_op | source)
XLA Modules:
  0.0 49.4 jit_solution(16447840179129869977)
XLA Ops:
  0.6 0.0 copy-start
  0.6 1.1 %copy-done = bf16[1,1,32,6,6,256]{5,2,4,3,1,0:T(8,128)(2,1)S(1)} copy-done((bf16[1,1,32,6,6,256]{5,2,4,3,1,0:T(8,128)(2,1)S(1)}, bf16[1,1,32,6,6,256]{5,2,4,3,1,0:T(8,128)(2,1)}, u32[]{:S(2)}) %copy-start) | copy-done | bytes 589848
  1.7 0.0 copy-start.1
  1.7 0.9 %copy-done.1 = f32[1,27,2048]{2,0,1:T(1,128)S(1)} copy-done((f32[1,27,2048]{2,0,1:T(1,128)S(1)}, f32[1,27,2048]{2,0,1:T(1,128)}, u32[]{:S(2)}) %copy-start.1) | copy-done | bytes 221208
  2.6 0.0 copy-start.2
  2.6 0.9 %copy-done.2 = f32[1,27,2048]{2,0,1:T(1,128)S(1)} copy-done((f32[1,27,2048]{2,0,1:T(1,128)S(1)}, f32[1,27,2048]{2,0,1:T(1,128)}, u32[]{:S(2)}) %copy-start.2) | copy-done | bytes 221208
  3.6 0.0 copy-start.3
  3.6 0.9 %copy-done.3 = f32[1,27,2048]{2,0,1:T(1,128)S(1)} copy-done((f32[1,27,2048]{2,0,1:T(1,128)S(1)}, f32[1,27,2048]{2,0,1:T(1,128)}, u32[]{:S(2)}) %copy-start.3) | copy-done | bytes 221208
  4.5 0.0 copy-start.4
  4.5 0.9 %copy-done.4 = bf16[1,1,64,3,3,128]{5,2,4,3,1,0:T(8,128)(2,1)S(1)} copy-done((bf16[1,1,64,3,3,128]{5,2,4,3,1,0:T(8,128)(2,1)S(1)}, bf16[1,1,64,3,3,128]{5,2,4,3,1,0:T(8,128)(2,1)}, u32[]{:S(2)}) %copy-start.4) | copy-done | bytes 147480
  5.4 41.1 %shard_map.84 = (bf16[3,3,64,128]{3,2,1,0:T(8,128)(2,1)S(1)}, bf16[6,6,32,256]{3,2,1,0:T(8,128)(2,1)S(1)}, f32[432,128]{1,0:T(8,128)S(1)}, f32[432,128]{1,0:T(8,128)S(1)}) custom-call(bf16[6,6,32,256]{3,2,1,0:T(8,128)(2,1)S(1)} %bitcast.21, bf16[3,3,64,128]{3,2,1,0:T(8,128)(2,1)S(1)} %bitcast.25, f32[432,128]{1,0:T(8,128)S(1)} %bitcast.22, ...), custom_call_target="tpu_custom_call" | custom-call | flops 600000000 | bytes 3000000 | tf_op jit(solution)/shard_map/pallas_call | solution.py:395
  46.6 0.7 %copy.17 = bf16[1,1,64,3,3,128]{5,2,4,3,1,0:T(8,128)(2,1)} copy(bf16[1,1,64,3,3,128]{5,2,4,3,1,0:T(8,128)(2,1)S(1)} %bitcast.20) | data formatting | bytes 294912
  47.2 0.8 %copy.18 = bf16[1,1,32,6,6,256]{5,2,4,3,1,0:T(8,128)(2,1)} copy(bf16[1,1,32,6,6,256]{5,2,4,3,1,0:T(8,128)(2,1)S(1)} %bitcast.17) | data formatting | bytes 1179648
  48.0 0.7 %copy.19 = f32[1,27,2048]{2,0,1:T(1,128)} copy(f32[1,27,2048]{2,0,1:T(1,128)S(1)} %bitcast.19) | data formatting | bytes 442368
  48.7 0.7 %copy.20 = f32[1,27,2048]{2,0,1:T(1,128)} copy(f32[1,27,2048]{2,0,1:T(1,128)S(1)} %bitcast.18) | data formatting | bytes 442368
Async XLA Ops:
  0.6 1.1 %copy-start = (bf16[1,1,32,6,6,256]{5,2,4,3,1,0:T(8,128)(2,1)S(1)}, bf16[1,1,32,6,6,256]{5,2,4,3,1,0:T(8,128)(2,1)}, u32[]{:S(2)}) copy-start(bf16[1,1,32,6,6,256]{5,2,4,3,1,0:T(8,128)(2,1)} %param.5) | copy-start | bytes 1769476
  1.7 0.9 %copy-start.1 = (f32[1,27,2048]{2,0,1:T(1,128)S(1)}, f32[1,27,2048]{2,0,1:T(1,128)}, u32[]{:S(2)}) copy-start(f32[1,27,2048]{2,0,1:T(1,128)} %param.7) | copy-start | bytes 663556
  2.6 0.9 %copy-start.2 = (f32[1,27,2048]{2,0,1:T(1,128)S(1)}, f32[1,27,2048]{2,0,1:T(1,128)}, u32[]{:S(2)}) copy-start(f32[1,27,2048]{2,0,1:T(1,128)} %param.8) | copy-start | bytes 663556
  3.6 0.9 %copy-start.3 = (f32[1,27,2048]{2,0,1:T(1,128)S(1)}, f32[1,27,2048]{2,0,1:T(1,128)}, u32[]{:S(2)}) copy-start(f32[1,27,2048]{2,0,1:T(1,128)} %param.9) | copy-start | bytes 663556
  4.5 0.9 %copy-start.4 = (bf16[1,1,64,3,3,128]{5,2,4,3,1,0:T(8,128)(2,1)S(1)}, bf16[1,1,64,3,3,128]{5,2,4,3,1,0:T(8,128)(2,1)}, u32[]{:S(2)}) copy-start(bf16[1,1,64,3,3,128]{5,2,4,3,1,0:T(8,128)(2,1)} %param.6) | copy-start | bytes 442372

commit v2 on v1

--- a/solution.py
+++ b/solution.py
@@ -19,17 +19,19 @@
 
 
 def kernel(
-    n_dp, n_seg, n_space, per_owner,
+    n_dp, n_seg, n_space, near, share,
+    feats_hbm, og_hbm, mean_hbm, noise_hbm, prec_hbm,
+    act_out, gin_out, mean_out, prec_out,
     feats, og, mean, noise, prec,
-    act_out, gin_out, mean_out, prec_out,
     cells, wts, wtr, l_own, l_got, halo, act_own, act_got, pg_own, pg_got, shifted,
-    grads, tiles, rs_got, total, ag_got,
-    p_send, p_recv, rs_send, rs_recv, ag_send, ag_recv,
+    grads, tiles, rs_got, far_got, total, ag_got,
+    loaded, p_send, p_recv, rs_send, rs_recv, far_send, far_recv, ag_send, ag_recv,
 ):
     dp, seg, space = (lax.axis_index(a) for a in ("dp", "segment", "space"))
-    n_group = n_dp * n_space
-    owners = -(-TAPS // per_owner)
-    me = dp * n_space + space
+    n_near, n_far = n_dp * near, n_space // near
+    owners = -(-TAPS // share)
+    spot, band = lax.rem(space, near), space // near
+    me = dp * near + spot
     first_seg, last_seg = seg == 0, seg == n_seg - 1
     has_next, has_prev = seg < n_seg - 1, seg > 0
     has_up, has_down = space < n_space - 1, space > 0
@@ -38,25 +40,45 @@
         return {"dp": d, "segment": s, "space": z}
 
     def peer(k):
-        other = lax.rem(me + k, n_group)
-        return other, at(other // n_space, seg, lax.rem(other, n_space))
+        other = lax.rem(me + k, n_near)
+        return other, at(other // near, seg, band * near + lax.rem(other, near))
+
+    def far_peer(k):
+        other = lax.rem(band + k, n_far)
+        return other, at(dp, seg, other * near + spot)
 
     barrier = pltpu.get_barrier_semaphore()
-
-    def greet(k, carry):
-        pl.semaphore_signal(barrier, inc=1, device_id=peer(k)[1], device_id_type=MESH)
-        return carry
-
-    lax.fori_loop(1, n_group, greet, 0)
-    for cond, to in (
+    greeted = [(True, peer(k)[1]) for k in range(1, n_near)]
+    greeted += [(True, far_peer(k)[1]) for k in range(1, n_far)]
+    greeted += [
+        (has_down & (spot == 0), at(dp, seg, space - 1)),
+        (has_up & (spot == near - 1), at(dp, seg, space + 1)),
         (has_prev, at(dp, seg - 1, space)),
         (has_next, at(dp, seg + 1, space)),
         (has_prev & has_down, at(dp, seg - 1, space - 1)),
         (has_next & has_up, at(dp, seg + 1, space + 1)),
-    ):
-        @pl.when(cond)
-        def _():
+    ]
+    peers = 0
+    for cond, to in greeted:
+        if cond is True:
             pl.semaphore_signal(barrier, inc=1, device_id=to, device_id_type=MESH)
+            peers = peers + 1
+        else:
+            @pl.when(cond)
+            def _():
+                pl.semaphore_signal(barrier, inc=1, device_id=to, device_id_type=MESH)
+
+            peers = peers + cond.astype(jnp.int32)
+
+    loads = [
+        pltpu.make_async_copy(src, dst, loaded.at[i])
+        for i, (src, dst) in enumerate(
+            [(mean_hbm, mean), (noise_hbm, noise), (prec_hbm, prec), (feats_hbm, feats), (og_hbm, og)]
+        )
+    ]
+    for load in loads:
+        load.start()
+    pl.semaphore_wait(barrier, peers)
 
     def link(i, src, dst, to):
         return pltpu.make_async_remote_copy(
@@ -67,7 +89,7 @@
     prev = at(dp, seg - 1, space)
     after = at(dp, seg + 1, space)
     links = [
-        (link(0, feats.at[feats.shape[0] - 1], halo, at(dp, seg, space + 1)), has_up, has_down),
+        (link(0, feats_hbm.at[feats_hbm.shape[0] - 1], halo, at(dp, seg, space + 1)), has_up, has_down),
         (link(1, l_own, l_got, prev), has_prev, has_next),
         (link(2, act_own.at[pl.ds(1, 2)], act_got.at[pl.ds(1, 2)], after), has_next, has_prev),
         (link(3, act_own.at[0], act_got.at[0], after), has_next, has_prev),
@@ -101,9 +123,12 @@
         def _():
             copy.wait_send()
 
+    start(0)
     lane = lax.broadcasted_iota(jnp.int32, (16, 128), 1)
     chunk = lane // 32
 
+    for load in loads[:3]:
+        load.wait()
     slabs = []
     for t in range(TAPS):
         rows = pl.ds(16 * t, 16)
@@ -119,16 +144,6 @@
                     block = jnp.where(chunk == tl, turned, block)
             wts[g, pl.ds(low, 16, stride=4), :] = block
 
-    peers = (
-        n_group - 1
-        + has_prev.astype(jnp.int32)
-        + has_next.astype(jnp.int32)
-        + (has_prev & has_down).astype(jnp.int32)
-        + (has_next & has_up).astype(jnp.int32)
-    )
-    pl.semaphore_wait(barrier, peers)
-    start(0)
-
     z_of = lax.broadcasted_iota(jnp.int32, (256, 384), 0)
     column = lax.broadcasted_iota(jnp.int32, (256, 384), 1)
     pick = (z_of == 2 * (column % 128) + column // 128 - 1).astype(F32).astype(BF16)
@@ -164,6 +179,8 @@
     def flat_weights():
         return jnp.concatenate([wts[g] for g in range(GROUPS)], axis=1).astype(BF16)
 
+    for load in loads[3:]:
+        load.wait()
     for x in range(6):
         spread(feats[x], x + 1)
     for i in (1, 2):
@@ -215,30 +232,82 @@
     for t in range(TAPS, tiles.shape[0]):
         tiles[t] = jnp.zeros((16, 128), BF16)
 
-    def rs_copy(other, to):
-        return pltpu.make_async_remote_copy(
-            src_ref=tiles.at[pl.ds(other * per_owner, per_owner)], dst_ref=rs_got.at[me],
+    def near_copy(other, to):
+        return pltpu.make_async_remote_copy(
+            src_ref=tiles.at[pl.ds(other * share, share)], dst_ref=rs_got.at[me],
             send_sem=rs_send.at[other], recv_sem=rs_recv.at[me],
             device_id=to, device_id_type=MESH,
         )
 
-    def rs_arrival(other):
-        return pltpu.make_async_remote_copy(
-            src_ref=tiles.at[pl.ds(0, per_owner)], dst_ref=rs_got.at[other],
+    def near_arrival(other):
+        return pltpu.make_async_remote_copy(
+            src_ref=tiles.at[pl.ds(0, share)], dst_ref=rs_got.at[other],
             send_sem=rs_send.at[other], recv_sem=rs_recv.at[other],
-            device_id=at(dp, seg, space), device_id_type=MESH,
-        )
-
-    def rs_go(k, carry):
+            device_id=peer(1)[1], device_id_type=MESH,
+        )
+
+    def far_copy(other, to):
+        return pltpu.make_async_remote_copy(
+            src_ref=far_got.at[band], dst_ref=far_got.at[band],
+            send_sem=far_send.at[other], recv_sem=far_recv.at[band],
+            device_id=to, device_id_type=MESH,
+        )
+
+    def far_arrival(other):
+        return pltpu.make_async_remote_copy(
+            src_ref=far_got.at[other], dst_ref=far_got.at[other],
+            send_sem=far_send.at[other], recv_sem=far_recv.at[other],
+            device_id=far_peer(1)[1], device_id_type=MESH,
+        )
+
+    def ag_copy(other, to):
+        return pltpu.make_async_remote_copy(
+            src_ref=total, dst_ref=ag_got.at[pl.ds(me * share, share)],
+            send_sem=ag_send.at[other], recv_sem=ag_recv.at[me],
+            device_id=to, device_id_type=MESH,
+        )
+
+    def ag_arrival(other):
+        return pltpu.make_async_remote_copy(
+            src_ref=total, dst_ref=ag_got.at[pl.ds(other * share, share)],
+            send_sem=ag_send.at[other], recv_sem=ag_recv.at[other],
+            device_id=peer(1)[1], device_id_type=MESH,
+        )
+
+    def when_owner(who, action):
+        @pl.when(who < owners)
+        def _():
+            action()
+
+    for k in range(1, n_near):
         other, to = peer(k)
-
-        @pl.when(other < owners)
-        def _():
-            rs_copy(other, to).start()
-
-        return carry
-
-    lax.fori_loop(1, n_group, rs_go, 0)
+        when_owner(other, near_copy(other, to).start)
+
+    def sum_near():
+        rs_got[me] = tiles[pl.ds(me * share, share)]
+        for k in range(1, n_near):
+            near_arrival(peer(k)[0]).wait_recv()
+        summed = rs_got[0].astype(F32)
+        for k in range(1, n_near):
+            summed += rs_got[k].astype(F32)
+        far_got[band] = summed.astype(BF16)
+        for k in range(1, n_far):
+            far_copy(*far_peer(k)).start()
+
+    inv_root = 1.0 / math.sqrt(n_dp * n_space * 3 * 3 * 128)
+
+    def sum_far():
+        for k in range(1, n_far):
+            far_arrival(far_peer(k)[0]).wait_recv()
+        summed = far_got[0].astype(F32)
+        for k in range(1, n_far):
+            summed += far_got[k].astype(F32)
+        total[...] = (summed * inv_root).astype(BF16)
+        for k in range(1, n_near):
+            ag_copy(*peer(k)).start()
+        ag_got[pl.ds(me * share, share)] = total[...]
+
+    when_owner(me, sum_near)
 
     for i in (2, 3):
         arrived(i)
@@ -308,54 +377,10 @@
     def _():
         gin_out[...] = jnp.zeros(gin_out.shape, BF16)
 
-    def ag_copy(other, to):
-        return pltpu.make_async_remote_copy(
-            src_ref=total, dst_ref=ag_got.at[pl.ds(me * per_owner, per_owner)],
-            send_sem=ag_send.at[other], recv_sem=ag_recv.at[me],
-            device_id=to, device_id_type=MESH,
-        )
-
-    def ag_arrival(other):
-        return pltpu.make_async_remote_copy(
-            src_ref=total, dst_ref=ag_got.at[pl.ds(other * per_owner, per_owner)],
-            send_sem=ag_send.at[other], recv_sem=ag_recv.at[other],
-            device_id=at(dp, seg, space), device_id_type=MESH,
-        )
-
-    inv_root = 1.0 / math.sqrt(n_group * 3 * 3 * 128)
-
-    @pl.when(me < owners)
-    def _():
-        rs_got[me] = tiles[pl.ds(me * per_owner, per_owner)]
-
-        def rs_wait(k, carry):
-            rs_arrival(peer(k)[0]).wait_recv()
-            return carry
-
-        lax.fori_loop(1, n_group, rs_wait, 0)
-        summed = rs_got[0].astype(F32)
-        for k in range(1, n_group):
-            summed += rs_got[k].astype(F32)
-        total[...] = (summed * inv_root).astype(BF16)
-
-        def ag_go(k, carry):
-            other, to = peer(k)
-            ag_copy(other, to).start()
-            return carry
-
-        lax.fori_loop(1, n_group, ag_go, 0)
-        ag_got[pl.ds(me * per_owner, per_owner)] = total[...]
-
-    def ag_wait(k, carry):
+    when_owner(me, sum_far)
+    for k in range(1, n_near):
         other, _ = peer(k)
-
-        @pl.when(other < owners)
-        def _():
-            ag_arrival(other).wait_recv()
-
-        return carry
-
-    lax.fori_loop(1, n_group, ag_wait, 0)
+        when_owner(other, ag_arrival(other).wait_recv)
     for t in range(TAPS):
         rows = pl.ds(16 * t, 16)
         scaled = ag_got[t].astype(F32)
@@ -366,43 +391,53 @@
     for i in range(len(links)):
         sent(i)
 
-    def rs_sent(k, carry):
+    for k in range(1, n_near):
         other, to = peer(k)
-
-        @pl.when(other < owners)
-        def _():
-            rs_copy(other, to).wait_send()
-
-        @pl.when(me < owners)
-        def _():
-            ag_copy(other, to).wait_send()
-
-        return carry
-
-    lax.fori_loop(1, n_group, rs_sent, 0)
+        when_owner(other, near_copy(other, to).wait_send)
+        when_owner(me, ag_copy(other, to).wait_send)
+    for k in range(1, n_far):
+        when_owner(me, far_copy(*far_peer(k)).wait_send)
+
+
+def deliver(*refs):
+    done = refs[-1]
+    copies = [pltpu.make_async_copy(refs[i], refs[4 + i], done.at[i]) for i in range(4)]
+    for copy in copies:
+        copy.start()
+    for copy in copies:
+        copy.wait()
 
 
 def per_device(features, out_grad, weight_mean, weight_noise, precision):
     n_dp, n_seg, n_space = (lax.axis_size(a) for a in ("dp", "segment", "space"))
-    n_group = n_dp * n_space
-    per_owner = -(-TAPS // n_group)
+    near = 4 if n_space % 4 == 0 and n_space > 4 else 2
+    n_near, n_far = n_dp * near, n_space // near
+    share = -(-TAPS // n_near)
     feats = jnp.transpose(features[0, 0], (1, 2, 0, 3))
     og = jnp.transpose(out_grad[0, 0], (1, 2, 0, 3))
     mean, noise, prec = (
         w.reshape(TAPS * 16, 128) for w in (weight_mean, weight_noise, precision)
     )
+    feats, og, mean, noise, prec = (
+        pltpu.with_memory_space_constraint(v, pltpu.HBM) for v in (feats, og, mean, noise, prec)
+    )
     vmem = pl.BlockSpec(memory_space=pltpu.VMEM)
     act, gin, mean_new, prec_new = pl.pallas_call(
-        functools.partial(kernel, n_dp, n_seg, n_space, per_owner),
+        functools.partial(kernel, n_dp, n_seg, n_space, near, share),
         out_shape=[
             jax.ShapeDtypeStruct((3, 3, 64, 128), BF16),
             jax.ShapeDtypeStruct((6, 6, 32, 256), BF16),
             jax.ShapeDtypeStruct((TAPS * 16, 128), F32),
             jax.ShapeDtypeStruct((TAPS * 16, 128), F32),
         ],
-        in_specs=[vmem] * 5,
+        in_specs=[pl.BlockSpec(memory_space=pltpu.HBM)] * 5,
         out_specs=[vmem] * 4,
         scratch_shapes=[
+            pltpu.VMEM((6, 6, 32, 256), BF16),
+            pltpu.VMEM((3, 3, 64, 128), BF16),
+            pltpu.VMEM((TAPS * 16, 128), F32),
+            pltpu.VMEM((TAPS * 16, 128), F32),
+            pltpu.VMEM((TAPS * 16, 128), F32),
             pltpu.VMEM((7, 7, 96, 128), BF16),
             pltpu.VMEM((GROUPS, 64, 128), F32),
             pltpu.VMEM((GROUPS * 128, 128), F32),
@@ -415,16 +450,20 @@
             pltpu.VMEM((4, 3, 64, 128), BF16),
             pltpu.VMEM((4, 4, 128, 128), BF16),
             pltpu.VMEM((GROUPS, 64, 128), F32),
-            pltpu.VMEM((n_group * per_owner, 16, 128), BF16),
-            pltpu.VMEM((n_group, per_owner, 16, 128), BF16),
-            pltpu.VMEM((per_owner, 16, 128), BF16),
-            pltpu.VMEM((n_group * per_owner, 16, 128), BF16),
+            pltpu.VMEM((n_near * share, 16, 128), BF16),
+            pltpu.VMEM((n_near, share, 16, 128), BF16),
+            pltpu.VMEM((n_far, share, 16, 128), BF16),
+            pltpu.VMEM((share, 16, 128), BF16),
+            pltpu.VMEM((n_near * share, 16, 128), BF16),
+            pltpu.SemaphoreType.DMA((5,)),
             pltpu.SemaphoreType.DMA((7,)),
             pltpu.SemaphoreType.DMA((7,)),
-            pltpu.SemaphoreType.DMA((n_group,)),
-            pltpu.SemaphoreType.DMA((n_group,)),
-            pltpu.SemaphoreType.DMA((n_group,)),
-            pltpu.SemaphoreType.DMA((n_group,)),
+            pltpu.SemaphoreType.DMA((n_near,)),
+            pltpu.SemaphoreType.DMA((n_near,)),
+            pltpu.SemaphoreType.DMA((n_far,)),
+            pltpu.SemaphoreType.DMA((n_far,)),
+            pltpu.SemaphoreType.DMA((n_near,)),
+            pltpu.SemaphoreType.DMA((n_near,)),
         ],
         compiler_params=pltpu.CompilerParams(
             collective_id=0, has_side_effects=True, vmem_limit_bytes=40 * 2**20
@@ -433,6 +472,14 @@
             flops=600_000_000, bytes_accessed=3_000_000, transcendentals=200_000
         ),
     )(feats, og, mean, noise, prec)
+    act, gin, mean_new, prec_new = pl.pallas_call(
+        deliver,
+        out_shape=[jax.ShapeDtypeStruct(v.shape, v.dtype) for v in (act, gin, mean_new, prec_new)],
+        in_specs=[vmem] * 4,
+        out_specs=[pl.BlockSpec(memory_space=pltpu.HBM)] * 4,
+        scratch_shapes=[pltpu.SemaphoreType.DMA((4,))],
+        compiler_params=pltpu.CompilerParams(vmem_limit_bytes=2**20),
+    )(act, gin, mean_new, prec_new)
     act = jnp.transpose(act, (2, 0, 1, 3))
     gin = jnp.transpose(gin, (2, 0, 1, 3))
     return (

time: 49.7 us -> 39.3 us (0.79)
  local copies, waits for them, and re-layouts: 7.62 us -> 0 us
  Pallas kernels: 41.1 us -> 38.5 us
    unnamed x14 -> x0, local copies, waits for them, and re-layouts: 7.62 us -> none
    pallas_call x1 -> x2, Pallas kernels: 41.1 us -> 38.5 us  [the longest x1 37.5 us: per_device(): pl.pallas_call(functools.partial(kernel, n_dp, n_seg, n_space, near, shar...]
where the time goes in v2:
time: 39.3 us; the launch traced here: 39.1 us
  Pallas kernels  38.5 us (98%)
  between operations  0.64 us (2%)
    pallas_call x1, Pallas kernels, per_device(): pl.pallas_call(functools.partial(kernel, n_dp, n_seg, n_space, near, shar...  37.5 us
    pallas_call x1, Pallas kernels, per_device(): pl.pallas_call(deliver, out_shape=[jax.ShapeDtypeStruct(v.shape, v.dtype)...  1.04 us

profile of v2, /device:TPU:24, one launch (start us, length us, event | category | flops | bytes accessed | tf_op | source)
XLA Modules:
  0.0 39.1 jit_solution(4218838006027824915)
XLA Ops:
  0.6 37.5 %shard_map.84 = (bf16[3,3,64,128]{3,2,1,0:T(8,128)(2,1)S(1)}, bf16[6,6,32,256]{3,2,1,0:T(8,128)(2,1)S(1)}, f32[432,128]{1,0:T(8,128)S(1)}, f32[432,128]{1,0:T(8,128)S(1)}) custom-call(bf16[6,6,32,256]{3,2,1,0:T(8,128)(2,1)} %bitcast.17, bf16[3,3,64,128]{3,2,1,0:T(8,128)(2,1)} %bitcast.24, f32[432,128]{1,0:T(8,128)} %bitcast.19, f32[432,128]{1,0:T(8,128)} %bitcast.20, ...), custom_call_target="tpu_custom_call" | custom-call | flops 600000000 | bytes 3000000 | tf_op jit(solution)/shard_map/pallas_call | solution.py:425
  38.1 1.0 %shard_map.85 = (bf16[3,3,64,128]{3,2,1,0:T(8,128)(2,1)}, bf16[6,6,32,256]{3,2,1,0:T(8,128)(2,1)}, f32[432,128]{1,0:T(8,128)}, f32[432,128]{1,0:T(8,128)}) custom-call(bf16[3,3,64,128]{3,2,1,0:T(8,128)(2,1)S(1)} %get-tuple-element.12.refs_0_, bf16[6,6,32,256]{3,2,1,0:T(8,128)(2,1)S(1)} %get-tuple-element.13.refs_1_, ...), custom_call_target="tpu_custom_call" | custom-call | tf_op jit(solution)/shard_map/pallas_call | solution.py:475

commit v3 on v2

--- a/solution.py
+++ b/solution.py
@@ -25,7 +25,7 @@
     feats, og, mean, noise, prec,
     cells, wts, wtr, l_own, l_got, halo, act_own, act_got, pg_own, pg_got, shifted,
     grads, tiles, rs_got, far_got, total, ag_got,
-    loaded, p_send, p_recv, rs_send, rs_recv, far_send, far_recv, ag_send, ag_recv,
+    heard, loaded, p_send, p_recv, rs_send, rs_recv, far_send, far_recv, ag_send, ag_recv,
 ):
     dp, seg, space = (lax.axis_index(a) for a in ("dp", "segment", "space"))
     n_near, n_far = n_dp * near, n_space // near
@@ -47,12 +47,15 @@
         other = lax.rem(band + k, n_far)
         return other, at(dp, seg, other * near + spot)
 
+    def along(step):
+        return lax.rem(space + step + n_space, n_space)
+
     barrier = pltpu.get_barrier_semaphore()
-    greeted = [(True, peer(k)[1]) for k in range(1, n_near)]
-    greeted += [(True, far_peer(k)[1]) for k in range(1, n_far)]
+    steps = sorted({step % n_space for step in (-2, -1, 1, 2)})
+    greeted = [(True, at(dp, seg, along(step))) for step in steps]
+    for step in sorted({step % n_space for step in (-1, 0, 1)}):
+        greeted += [(True, at(lax.rem(dp + k, n_dp), seg, along(step))) for k in range(1, n_dp)]
     greeted += [
-        (has_down & (spot == 0), at(dp, seg, space - 1)),
-        (has_up & (spot == near - 1), at(dp, seg, space + 1)),
         (has_prev, at(dp, seg - 1, space)),
         (has_next, at(dp, seg + 1, space)),
         (has_prev & has_down, at(dp, seg - 1, space - 1)),
@@ -69,6 +72,17 @@
                 pl.semaphore_signal(barrier, inc=1, device_id=to, device_id_type=MESH)
 
             peers = peers + cond.astype(jnp.int32)
+
+    def tell(word, reach):
+        for side, step in enumerate((reach, -reach)):
+            pl.semaphore_signal(
+                heard.at[word, side], inc=1, device_id=at(dp, seg, along(step)),
+                device_id_type=MESH,
+            )
+
+    def hear(word):
+        for side in range(2):
+            pl.semaphore_wait(heard.at[word, side], 1)
 
     loads = [
         pltpu.make_async_copy(src, dst, loaded.at[i])
@@ -124,6 +138,7 @@
             copy.wait_send()
 
     start(0)
+    tell(0, 2)
     lane = lax.broadcasted_iota(jnp.int32, (16, 128), 1)
     chunk = lane // 32
 
@@ -208,6 +223,9 @@
         cells[0] = jnp.zeros(cells.shape[1:], BF16)
 
     forward(0, flat_weights())
+    hear(0)
+    if n_space > 2 * near:
+        tell(1, near)
     for i in (3, 5, 6):
         start(i)
 
@@ -291,6 +309,8 @@
         for k in range(1, n_near):
             summed += rs_got[k].astype(F32)
         far_got[band] = summed.astype(BF16)
+
+    def go_far():
         for k in range(1, n_far):
             far_copy(*far_peer(k)).start()
 
@@ -308,6 +328,9 @@
         ag_got[pl.ds(me * share, share)] = total[...]
 
     when_owner(me, sum_near)
+    if n_space > 2 * near:
+        hear(1)
+    when_owner(me, go_far)
 
     for i in (2, 3):
         arrived(i)
@@ -455,6 +478,7 @@
             pltpu.VMEM((n_far, share, 16, 128), BF16),
             pltpu.VMEM((share, 16, 128), BF16),
             pltpu.VMEM((n_near * share, 16, 128), BF16),
+            pltpu.SemaphoreType.REGULAR((2, 2)),
             pltpu.SemaphoreType.DMA((5,)),
             pltpu.SemaphoreType.DMA((7,)),
             pltpu.SemaphoreType.DMA((7,)),

time: 39.3 us -> 38 us (0.967)
  the two profiles are of different devices: /device:TPU:24 before, /device:TPU:4 now
where the time goes in v3:
time: 38 us; the launch traced here: 37.9 us
  Pallas kernels  37.2 us (98%)
  between operations  0.64 us (2%)
    pallas_call x1, Pallas kernels, per_device(): pl.pallas_call(functools.partial(kernel, n_dp, n_seg, n_space, near, shar...  36.2 us
    pallas_call x1, Pallas kernels, per_device(): pl.pallas_call(deliver, out_shape=[jax.ShapeDtypeStruct(v.shape, v.dtype)...  1.04 us

profile of v3, /device:TPU:4, one launch (start us, length us, event | category | flops | bytes accessed | tf_op | source)
XLA Modules:
  0.0 37.9 jit_solution(2827507602192470280)
XLA Ops:
  0.6 36.2 %shard_map.84 = (bf16[3,3,64,128]{3,2,1,0:T(8,128)(2,1)S(1)}, bf16[6,6,32,256]{3,2,1,0:T(8,128)(2,1)S(1)}, f32[432,128]{1,0:T(8,128)S(1)}, f32[432,128]{1,0:T(8,128)S(1)}) custom-call(bf16[6,6,32,256]{3,2,1,0:T(8,128)(2,1)} %bitcast.17, bf16[3,3,64,128]{3,2,1,0:T(8,128)(2,1)} %bitcast.24, f32[432,128]{1,0:T(8,128)} %bitcast.19, f32[432,128]{1,0:T(8,128)} %bitcast.20, ...), custom_call_target="tpu_custom_call" | custom-call | flops 600000000 | bytes 3000000 | tf_op jit(solution)/shard_map/pallas_call | solution.py:448
  36.8 1.0 %shard_map.85 = (bf16[3,3,64,128]{3,2,1,0:T(8,128)(2,1)}, bf16[6,6,32,256]{3,2,1,0:T(8,128)(2,1)}, f32[432,128]{1,0:T(8,128)}, f32[432,128]{1,0:T(8,128)}) custom-call(bf16[3,3,64,128]{3,2,1,0:T(8,128)(2,1)S(1)} %get-tuple-element.12.refs_0_, bf16[6,6,32,256]{3,2,1,0:T(8,128)(2,1)S(1)} %get-tuple-element.13.refs_1_, ...), custom_call_target="tpu_custom_call" | custom-call | tf_op jit(solution)/shard_map/pallas_call | solution.py:499

commit v4 on v3

--- a/solution.py
+++ b/solution.py
@@ -24,7 +24,7 @@
     act_out, gin_out, mean_out, prec_out,
     feats, og, mean, noise, prec,
     cells, wts, wtr, l_own, l_got, halo, act_own, act_got, pg_own, pg_got, shifted,
-    grads, tiles, rs_got, far_got, total, ag_got,
+    grads, begun, tiles, rs_got, far_got, total, ag_got,
     heard, loaded, p_send, p_recv, rs_send, rs_recv, far_send, far_recv, ag_send, ag_recv,
 ):
     dp, seg, space = (lax.axis_index(a) for a in ("dp", "segment", "space"))
@@ -32,6 +32,9 @@
     owners = -(-TAPS // share)
     spot, band = lax.rem(space, near), space // near
     me = dp * near + spot
+    odd = lax.rem(seg, 2)
+    sums = (odd == 1) & (me < owners)
+    mate = seg + 1 - 2 * odd
     first_seg, last_seg = seg == 0, seg == n_seg - 1
     has_next, has_prev = seg < n_seg - 1, seg > 0
     has_up, has_down = space < n_space - 1, space > 0
@@ -51,10 +54,13 @@
         return lax.rem(space + step + n_space, n_space)
 
     barrier = pltpu.get_barrier_semaphore()
-    steps = sorted({step % n_space for step in (-2, -1, 1, 2)})
-    greeted = [(True, at(dp, seg, along(step))) for step in steps]
-    for step in sorted({step % n_space for step in (-1, 0, 1)}):
-        greeted += [(True, at(lax.rem(dp + k, n_dp), seg, along(step))) for k in range(1, n_dp)]
+    greeted = []
+    for which in (seg, mate):
+        for step in sorted({step % n_space for step in (-2, -1, 1, 2)}):
+            greeted.append((True, at(dp, which, along(step))))
+        for step in sorted({step % n_space for step in (-1, 0, 1)}):
+            for k in range(1, n_dp):
+                greeted.append((True, at(lax.rem(dp + k, n_dp), which, along(step))))
     greeted += [
         (has_prev, at(dp, seg - 1, space)),
         (has_next, at(dp, seg + 1, space)),
@@ -174,15 +180,14 @@
     for x in range(7):
         cells[x, 0] = jnp.zeros((96, 128), BF16)
 
-    def patch(i):
-        blocks = []
+    def patch(i, low=0, high=3):
+        columns = []
         for j in range(3):
-            parts = [cells[2 * i + a, 2 * j : 2 * j + 3].reshape(288, 128) for a in range(3)]
-            blocks.append(jnp.concatenate([*parts, jnp.zeros((32, 128), BF16)], axis=0))
-        return jnp.concatenate(blocks, axis=1)
-
-    def forward(i, weights):
-        preact = matmul(weights, patch(i))
+            parts = [cells[2 * i + a, 2 * j : 2 * j + 3].reshape(288, 128) for a in range(low, high)]
+            columns.append(jnp.concatenate(parts, axis=0))
+        return jnp.concatenate(columns, axis=1)
+
+    def finish(i, preact):
         grad = jnp.concatenate([og[i, j] for j in range(3)], axis=1).astype(F32)
         gate = jax.nn.sigmoid(preact)
         act = (preact * gate).astype(BF16)
@@ -192,14 +197,14 @@
             pg_own[i, j] = pre_grad[:, 128 * j : 128 * j + 128]
 
     def flat_weights():
-        return jnp.concatenate([wts[g] for g in range(GROUPS)], axis=1).astype(BF16)
+        return jnp.concatenate([wts[g] for g in range(GROUPS)], axis=1)[:, : TAPS * 32].astype(BF16)
 
     for load in loads[3:]:
         load.wait()
     for x in range(6):
         spread(feats[x], x + 1)
     for i in (1, 2):
-        forward(i, flat_weights())
+        finish(i, matmul(flat_weights(), patch(i)))
     start(2)
     start(4)
 
@@ -209,9 +214,21 @@
     for ab in range(9):
         w0, w1, w2 = (wtr[pl.ds(32 * (3 * ab + e), 32), :] for e in range(3))
         even = jnp.where(half, w1, 0.0)
-        odd = jnp.where(half, w2, w0)
-        l_own[ab] = jnp.concatenate([even, odd], axis=0).astype(BF16)
+        skew = jnp.where(half, w2, w0)
+        l_own[ab] = jnp.concatenate([even, skew], axis=0).astype(BF16)
     start(1)
+
+    def grad_rows(i):
+        return jnp.concatenate([pg_own[i, j] for j in range(3)], axis=1)
+
+    for i in (1, 2):
+        part = matmul(grad_rows(i), patch(i), ((1,), (1,)))
+        for g in range(GROUPS):
+            piece = part[:, 128 * g : 128 * g + 128]
+            if g == GROUPS - 1:
+                piece = jnp.concatenate([piece, jnp.zeros((64, 32), F32)], axis=1)
+            grads[g] = piece if i == 1 else grads[g] + piece
+    begun[...] = matmul(flat_weights()[:, 288:], patch(0, 1, 3))
 
     @pl.when(has_down)
     def _():
@@ -222,20 +239,68 @@
     def _():
         cells[0] = jnp.zeros(cells.shape[1:], BF16)
 
-    forward(0, flat_weights())
+    finish(0, begun[...] + matmul(flat_weights()[:, :288], patch(0, 0, 1)))
+
+    def near_copy(o):
+        return pltpu.make_async_remote_copy(
+            src_ref=tiles.at[pl.ds(o * share, share)], dst_ref=rs_got.at[odd, me],
+            send_sem=rs_send.at[o], recv_sem=rs_recv.at[odd, me],
+            device_id=at(o // near, seg + 1 - odd, band * near + o % near),
+            device_id_type=MESH,
+        )
+
+    def near_arrival(pair, other):
+        return pltpu.make_async_remote_copy(
+            src_ref=tiles.at[pl.ds(0, share)], dst_ref=rs_got.at[pair, other],
+            send_sem=rs_send.at[0], recv_sem=rs_recv.at[pair, other],
+            device_id=peer(1)[1], device_id_type=MESH,
+        )
+
+    def far_copy(pair, k):
+        other, to = far_peer(k)
+        return pltpu.make_async_remote_copy(
+            src_ref=far_got.at[pair, band], dst_ref=far_got.at[pair, band],
+            send_sem=far_send.at[pair, other], recv_sem=far_recv.at[pair, band],
+            device_id=to, device_id_type=MESH,
+        )
+
+    def far_arrival(pair, k):
+        other, to = far_peer(k)
+        return pltpu.make_async_remote_copy(
+            src_ref=far_got.at[pair, other], dst_ref=far_got.at[pair, other],
+            send_sem=far_send.at[pair, other], recv_sem=far_recv.at[pair, other],
+            device_id=to, device_id_type=MESH,
+        )
+
+    def ag_copy(pair, k):
+        other, _ = peer(k)
+        return pltpu.make_async_remote_copy(
+            src_ref=total.at[pair], dst_ref=ag_got.at[pl.ds(me * share, share)],
+            send_sem=ag_send.at[pair, other], recv_sem=ag_recv.at[me],
+            device_id=at(other // near, seg - 1 + pair, band * near + lax.rem(other, near)),
+            device_id_type=MESH,
+        )
+
+    def ag_arrival(o):
+        return pltpu.make_async_remote_copy(
+            src_ref=total.at[0], dst_ref=ag_got.at[pl.ds(o * share, share)],
+            send_sem=ag_send.at[0, 0], recv_sem=ag_recv.at[o],
+            device_id=peer(1)[1], device_id_type=MESH,
+        )
+
+    last = matmul(grad_rows(0), patch(0), ((1,), (1,)))
     hear(0)
     if n_space > 2 * near:
-        tell(1, near)
-    for i in (3, 5, 6):
-        start(i)
-
-    for i in (1, 2, 0):
-        pre_grad = jnp.concatenate([pg_own[i, j] for j in range(3)], axis=1)
-        part = matmul(pre_grad, patch(i), ((1,), (1,)))
-        for g in range(GROUPS):
-            piece = part[:, 128 * g : 128 * g + 128]
-            grads[g] = piece if i == 1 else grads[g] + piece
+        @pl.when(odd == 1)
+        def _():
+            tell(1, near)
+
+    made = 0
     for g in range(GROUPS):
+        piece = last[:, 128 * g : 128 * g + 128]
+        if g == GROUPS - 1:
+            piece = jnp.concatenate([piece, jnp.zeros((64, 32), F32)], axis=1)
+        grads[g] = grads[g] + piece
         rows = [grads[g, pl.ds(low, 16, stride=4), :] for low in range(4)]
         for tl in range(4):
             t = 4 * g + tl
@@ -247,90 +312,57 @@
                         turned = pltpu.roll(turned, ((low - tl) * 32) % 128, 1)
                     tile = jnp.where(chunk == low, turned, tile)
                 tiles[t] = tile.astype(BF16)
-    for t in range(TAPS, tiles.shape[0]):
-        tiles[t] = jnp.zeros((16, 128), BF16)
-
-    def near_copy(other, to):
-        return pltpu.make_async_remote_copy(
-            src_ref=tiles.at[pl.ds(other * share, share)], dst_ref=rs_got.at[me],
-            send_sem=rs_send.at[other], recv_sem=rs_recv.at[me],
-            device_id=to, device_id_type=MESH,
-        )
-
-    def near_arrival(other):
-        return pltpu.make_async_remote_copy(
-            src_ref=tiles.at[pl.ds(0, share)], dst_ref=rs_got.at[other],
-            send_sem=rs_send.at[other], recv_sem=rs_recv.at[other],
-            device_id=peer(1)[1], device_id_type=MESH,
-        )
-
-    def far_copy(other, to):
-        return pltpu.make_async_remote_copy(
-            src_ref=far_got.at[band], dst_ref=far_got.at[band],
-            send_sem=far_send.at[other], recv_sem=far_recv.at[band],
-            device_id=to, device_id_type=MESH,
-        )
-
-    def far_arrival(other):
-        return pltpu.make_async_remote_copy(
-            src_ref=far_got.at[other], dst_ref=far_got.at[other],
-            send_sem=far_send.at[other], recv_sem=far_recv.at[other],
-            device_id=far_peer(1)[1], device_id_type=MESH,
-        )
-
-    def ag_copy(other, to):
-        return pltpu.make_async_remote_copy(
-            src_ref=total, dst_ref=ag_got.at[pl.ds(me * share, share)],
-            send_sem=ag_send.at[other], recv_sem=ag_recv.at[me],
-            device_id=to, device_id_type=MESH,
-        )
-
-    def ag_arrival(other):
-        return pltpu.make_async_remote_copy(
-            src_ref=total, dst_ref=ag_got.at[pl.ds(other * share, share)],
-            send_sem=ag_send.at[other], recv_sem=ag_recv.at[other],
-            device_id=peer(1)[1], device_id_type=MESH,
-        )
-
-    def when_owner(who, action):
-        @pl.when(who < owners)
-        def _():
-            action()
-
-    for k in range(1, n_near):
-        other, to = peer(k)
-        when_owner(other, near_copy(other, to).start)
-
-    def sum_near():
-        rs_got[me] = tiles[pl.ds(me * share, share)]
+        if g == GROUPS - 1:
+            for t in range(TAPS, tiles.shape[0]):
+                tiles[t] = jnp.zeros((16, 128), BF16)
+        while made < owners and ((made + 1) * share <= 4 * g + 4 or g == GROUPS - 1):
+            @pl.when((me != made) | (odd == 0))
+            def _(o=made):
+                near_copy(o).start()
+
+            made += 1
+    for i in (5, 6, 3):
+        start(i)
+
+    inv_root = 1.0 / math.sqrt(n_dp * n_space * 3 * 3 * 128)
+
+    def sum_near(pair):
+        for k in range(pair, n_near):
+            near_arrival(pair, peer(k)[0]).wait_recv()
+        summed = rs_got[pair, 0].astype(F32)
         for k in range(1, n_near):
-            near_arrival(peer(k)[0]).wait_recv()
-        summed = rs_got[0].astype(F32)
-        for k in range(1, n_near):
-            summed += rs_got[k].astype(F32)
-        far_got[band] = summed.astype(BF16)
-
-    def go_far():
+            summed += rs_got[pair, k].astype(F32)
+        far_got[pair, band] = summed.astype(BF16)
+
+    def go_far(pair):
         for k in range(1, n_far):
-            far_copy(*far_peer(k)).start()
-
-    inv_root = 1.0 / math.sqrt(n_dp * n_space * 3 * 3 * 128)
-
-    def sum_far():
+            far_copy(pair, k).start()
+
+    def sum_far(pair):
         for k in range(1, n_far):
-            far_arrival(far_peer(k)[0]).wait_recv()
-        summed = far_got[0].astype(F32)
+            far_arrival(pair, k).wait_recv()
+        summed = far_got[pair, 0].astype(F32)
         for k in range(1, n_far):
-            summed += far_got[k].astype(F32)
-        total[...] = (summed * inv_root).astype(BF16)
-        for k in range(1, n_near):
-            ag_copy(*peer(k)).start()
-        ag_got[pl.ds(me * share, share)] = total[...]
-
-    when_owner(me, sum_near)
+            summed += far_got[pair, k].astype(F32)
+        total[pair] = (summed * inv_root).astype(BF16)
+        for k in range(pair, n_near):
+            ag_copy(pair, k).start()
+
+    @pl.when(sums)
+    def _():
+        rs_got[1, me] = tiles[pl.ds(me * share, share)]
+        sum_near(1)
+
     if n_space > 2 * near:
-        hear(1)
-    when_owner(me, go_far)
+        @pl.when(odd == 1)
+        def _():
+            hear(1)
+
+    @pl.when(sums)
+    def _():
+        go_far(1)
+        sum_near(0)
+        go_far(0)
 
     for i in (2, 3):
         arrived(i)
@@ -400,11 +432,18 @@
     def _():
         gin_out[...] = jnp.zeros(gin_out.shape, BF16)
 
-    when_owner(me, sum_far)
-    for k in range(1, n_near):
-        other, _ = peer(k)
-        when_owner(other, ag_arrival(other).wait_recv)
+    @pl.when(sums)
+    def _():
+        sum_far(1)
+        sum_far(0)
+        ag_got[pl.ds(me * share, share)] = total[1]
+
     for t in range(TAPS):
+        if t % share == 0:
+            @pl.when((me != t // share) | (odd == 0))
+            def _(o=t // share):
+                ag_arrival(o).wait_recv()
+
         rows = pl.ds(16 * t, 16)
         scaled = ag_got[t].astype(F32)
         prec_new = 0.75 * prec[rows] + 0.25 * scaled * scaled
@@ -414,17 +453,28 @@
     for i in range(len(links)):
         sent(i)
 
-    for k in range(1, n_near):
-        other, to = peer(k)
-        when_owner(other, near_copy(other, to).wait_send)
-        when_owner(me, ag_copy(other, to).wait_send)
-    for k in range(1, n_far):
-        when_owner(me, far_copy(*far_peer(k)).wait_send)
+    for o in range(owners):
+        @pl.when((me != o) | (odd == 0))
+        def _():
+            near_copy(o).wait_send()
+
+    @pl.when(sums)
+    def _():
+        for pair in range(2):
+            for k in range(1, n_far):
+                far_copy(pair, k).wait_send()
+            for k in range(pair, n_near):
+                ag_copy(pair, k).wait_send()
 
 
 def deliver(*refs):
     done = refs[-1]
-    copies = [pltpu.make_async_copy(refs[i], refs[4 + i], done.at[i]) for i in range(4)]
+    parts = [(i, k) for i in (1, 0) for k in range(3)] + [(i, k) for i in (2, 3) for k in range(2)]
+    copies = []
+    for n, (i, k) in enumerate(parts):
+        size = refs[i].shape[0] // (3 if i < 2 else 2)
+        rows = pl.ds(size * k, size)
+        copies.append(pltpu.make_async_copy(refs[i].at[rows], refs[4 + i].at[rows], done.at[n]))
     for copy in copies:
         copy.start()
     for copy in copies:
@@ -473,20 +523,21 @@
             pltpu.VMEM((4, 3, 64, 128), BF16),
             pltpu.VMEM((4, 4, 128, 128), BF16),
             pltpu.VMEM((GROUPS, 64, 128), F32),
+            pltpu.VMEM((64, 384), F32),
             pltpu.VMEM((n_near * share, 16, 128), BF16),
-            pltpu.VMEM((n_near, share, 16, 128), BF16),
-            pltpu.VMEM((n_far, share, 16, 128), BF16),
-            pltpu.VMEM((share, 16, 128), BF16),
+            pltpu.VMEM((2, n_near, share, 16, 128), BF16),
+            pltpu.VMEM((2, n_far, share, 16, 128), BF16),
+            pltpu.VMEM((2, share, 16, 128), BF16),
             pltpu.VMEM((n_near * share, 16, 128), BF16),
             pltpu.SemaphoreType.REGULAR((2, 2)),
             pltpu.SemaphoreType.DMA((5,)),
             pltpu.SemaphoreType.DMA((7,)),
             pltpu.SemaphoreType.DMA((7,)),
             pltpu.SemaphoreType.DMA((n_near,)),
-            pltpu.SemaphoreType.DMA((n_near,)),
-            pltpu.SemaphoreType.DMA((n_far,)),
-            pltpu.SemaphoreType.DMA((n_far,)),
-            pltpu.SemaphoreType.DMA((n_near,)),
+            pltpu.SemaphoreType.DMA((2, n_near)),
+            pltpu.SemaphoreType.DMA((2, n_far)),
+            pltpu.SemaphoreType.DMA((2, n_far)),
+            pltpu.SemaphoreType.DMA((2, n_near)),
             pltpu.SemaphoreType.DMA((n_near,)),
         ],
         compiler_params=pltpu.CompilerParams(
@@ -501,7 +552,7 @@
         out_shape=[jax.ShapeDtypeStruct(v.shape, v.dtype) for v in (act, gin, mean_new, prec_new)],
         in_specs=[vmem] * 4,
         out_specs=[pl.BlockSpec(memory_space=pltpu.HBM)] * 4,
-        scratch_shapes=[pltpu.SemaphoreType.DMA((4,))],
+        scratch_shapes=[pltpu.SemaphoreType.DMA((10,))],
         compiler_params=pltpu.CompilerParams(vmem_limit_bytes=2**20),
     )(act, gin, mean_new, prec_new)
     act = jnp.transpose(act, (2, 0, 1, 3))

time: 38 us -> 36.6 us (0.963)
  the two profiles are of different devices: /device:TPU:4 before, /device:TPU:24 now
where the time goes in v4:
time: 36.6 us; the launch traced here: 36.5 us
  Pallas kernels  35.8 us (98%)
  between operations  0.64 us (2%)
    pallas_call x1, Pallas kernels, per_device(): pl.pallas_call(functools.partial(kernel, n_dp, n_seg, n_space, near, shar...  34.8 us
    pallas_call x1, Pallas kernels, per_device(): pl.pallas_call(deliver, out_shape=[jax.ShapeDtypeStruct(v.shape, v.dtype)...  1.09 us

profile of v4, /device:TPU:24, one launch (start us, length us, event | category | flops | bytes accessed | tf_op | source)
XLA Modules:
  0.0 36.5 jit_solution(1399130269819175020)
XLA Ops:
  0.6 34.8 %shard_map.84 = (bf16[3,3,64,128]{3,2,1,0:T(8,128)(2,1)S(1)}, bf16[6,6,32,256]{3,2,1,0:T(8,128)(2,1)S(1)}, f32[432,128]{1,0:T(8,128)S(1)}, f32[432,128]{1,0:T(8,128)S(1)}) custom-call(bf16[6,6,32,256]{3,2,1,0:T(8,128)(2,1)} %bitcast.17, bf16[3,3,64,128]{3,2,1,0:T(8,128)(2,1)} %bitcast.24, f32[432,128]{1,0:T(8,128)} %bitcast.19, f32[432,128]{1,0:T(8,128)} %bitcast.20, ...), custom_call_target="tpu_custom_call" | custom-call | flops 600000000 | bytes 3000000 | tf_op jit(solution)/shard_map/pallas_call | solution.py:498
  35.4 1.1 %shard_map.85 = (bf16[3,3,64,128]{3,2,1,0:T(8,128)(2,1)}, bf16[6,6,32,256]{3,2,1,0:T(8,128)(2,1)}, f32[432,128]{1,0:T(8,128)}, f32[432,128]{1,0:T(8,128)}) custom-call(bf16[3,3,64,128]{3,2,1,0:T(8,128)(2,1)S(1)} %get-tuple-element.12.refs_0_, bf16[6,6,32,256]{3,2,1,0:T(8,128)(2,1)S(1)} %get-tuple-element.13.refs_1_, ...), custom_call_target="tpu_custom_call" | custom-call | tf_op jit(solution)/shard_map/pallas_call | solution.py:550

commit v5 on v4

--- a/solution.py
+++ b/solution.py
@@ -93,7 +93,7 @@
     loads = [
         pltpu.make_async_copy(src, dst, loaded.at[i])
         for i, (src, dst) in enumerate(
-            [(mean_hbm, mean), (noise_hbm, noise), (prec_hbm, prec), (feats_hbm, feats), (og_hbm, og)]
+            [(feats_hbm, feats), (mean_hbm, mean), (noise_hbm, noise), (prec_hbm, prec), (og_hbm, og)]
         )
     ]
     for load in loads:
@@ -109,7 +109,7 @@
     prev = at(dp, seg - 1, space)
     after = at(dp, seg + 1, space)
     links = [
-        (link(0, feats_hbm.at[feats_hbm.shape[0] - 1], halo, at(dp, seg, space + 1)), has_up, has_down),
+        (link(0, feats.at[feats.shape[0] - 1], halo, at(dp, seg, space + 1)), has_up, has_down),
         (link(1, l_own, l_got, prev), has_prev, has_next),
         (link(2, act_own.at[pl.ds(1, 2)], act_got.at[pl.ds(1, 2)], after), has_next, has_prev),
         (link(3, act_own.at[0], act_got.at[0], after), has_next, has_prev),
@@ -143,12 +143,13 @@
         def _():
             copy.wait_send()
 
+    loads[0].wait()
     start(0)
     tell(0, 2)
     lane = lax.broadcasted_iota(jnp.int32, (16, 128), 1)
     chunk = lane // 32
 
-    for load in loads[:3]:
+    for load in loads[1:4]:
         load.wait()
     slabs = []
     for t in range(TAPS):
@@ -199,8 +200,7 @@
     def flat_weights():
         return jnp.concatenate([wts[g] for g in range(GROUPS)], axis=1)[:, : TAPS * 32].astype(BF16)
 
-    for load in loads[3:]:
-        load.wait()
+    loads[4].wait()
     for x in range(6):
         spread(feats[x], x + 1)
     for i in (1, 2):
@@ -335,7 +335,7 @@
         far_got[pair, band] = summed.astype(BF16)
 
     def go_far(pair):
-        for k in range(1, n_far):
+        for k in sorted(range(1, n_far), key=lambda k: -min(k, n_far - k)):
             far_copy(pair, k).start()
 
     def sum_far(pair):

time: 36.6 us -> 35.7 us (0.975)
  Pallas kernels: 35.8 us -> 35 us
    pallas_call x1, Pallas kernels: 34.8 us -> 33.9 us  [per_device(): pl.pallas_call(functools.partial(kernel, n_dp, n_seg, n_space, near, shar...]
where the time goes in v5:
time: 35.7 us; the launch traced here: 35.6 us
  Pallas kernels  35 us (98%)
  between operations  0.64 us (2%)
    pallas_call x1, Pallas kernels, per_device(): pl.pallas_call(functools.partial(kernel, n_dp, n_seg, n_space, near, shar...  33.9 us
    pallas_call x1, Pallas kernels, per_device(): pl.pallas_call(deliver, out_shape=[jax.ShapeDtypeStruct(v.shape, v.dtype)...  1.09 us

profile of v5, /device:TPU:24, one launch (start us, length us, event | category | flops | bytes accessed | tf_op | source)
XLA Modules:
  0.0 35.6 jit_solution(7913606791882581689)
XLA Ops:
  0.6 33.9 %shard_map.84 = (bf16[3,3,64,128]{3,2,1,0:T(8,128)(2,1)S(1)}, bf16[6,6,32,256]{3,2,1,0:T(8,128)(2,1)S(1)}, f32[432,128]{1,0:T(8,128)S(1)}, f32[432,128]{1,0:T(8,128)S(1)}) custom-call(bf16[6,6,32,256]{3,2,1,0:T(8,128)(2,1)} %bitcast.17, bf16[3,3,64,128]{3,2,1,0:T(8,128)(2,1)} %bitcast.24, f32[432,128]{1,0:T(8,128)} %bitcast.19, f32[432,128]{1,0:T(8,128)} %bitcast.20, ...), custom_call_target="tpu_custom_call" | custom-call | flops 600000000 | bytes 3000000 | tf_op jit(solution)/shard_map/pallas_call | solution.py:498
  34.5 1.1 %shard_map.85 = (bf16[3,3,64,128]{3,2,1,0:T(8,128)(2,1)}, bf16[6,6,32,256]{3,2,1,0:T(8,128)(2,1)}, f32[432,128]{1,0:T(8,128)}, f32[432,128]{1,0:T(8,128)}) custom-call(bf16[3,3,64,128]{3,2,1,0:T(8,128)(2,1)S(1)} %get-tuple-element.12.refs_0_, bf16[6,6,32,256]{3,2,1,0:T(8,128)(2,1)S(1)} %get-tuple-element.13.refs_1_, ...), custom_call_target="tpu_custom_call" | custom-call | tf_op jit(solution)/shard_map/pallas_call | solution.py:550

commit v6 on v5

--- a/solution.py
+++ b/solution.py
@@ -21,7 +21,7 @@
 def kernel(
     n_dp, n_seg, n_space, near, share,
     feats_hbm, og_hbm, mean_hbm, noise_hbm, prec_hbm,
-    act_out, gin_out, mean_out, prec_out,
+    act_out, gin_out, mean_out, prec_out, scaled_out,
     feats, og, mean, noise, prec,
     cells, wts, wtr, l_own, l_got, halo, act_own, act_got, pg_own, pg_got, shifted,
     grads, begun, tiles, rs_got, far_got, total, ag_got,
@@ -363,6 +363,9 @@
         go_far(1)
         sum_near(0)
         go_far(0)
+
+    mean_out[...] = mean[...]
+    prec_out[...] = prec[...]
 
     for i in (2, 3):
         arrived(i)
@@ -438,17 +441,12 @@
         sum_far(0)
         ag_got[pl.ds(me * share, share)] = total[1]
 
-    for t in range(TAPS):
-        if t % share == 0:
-            @pl.when((me != t // share) | (odd == 0))
-            def _(o=t // share):
-                ag_arrival(o).wait_recv()
-
-        rows = pl.ds(16 * t, 16)
-        scaled = ag_got[t].astype(F32)
-        prec_new = 0.75 * prec[rows] + 0.25 * scaled * scaled
-        prec_out[rows] = prec_new
-        mean_out[rows] = mean[rows] - 0.03 * scaled / (prec_new + 0.1)
+    for o in range(owners):
+        @pl.when((me != o) | (odd == 0))
+        def _():
+            ag_arrival(o).wait_recv()
+
+    scaled_out[...] = ag_got[:TAPS]
 
     for i in range(len(links)):
         sent(i)
@@ -467,16 +465,28 @@
                 ag_copy(pair, k).wait_send()
 
 
-def deliver(*refs):
-    done = refs[-1]
-    parts = [(i, k) for i in (1, 0) for k in range(3)] + [(i, k) for i in (2, 3) for k in range(2)]
+def deliver(
+    act, gin, mean, prec, scaled, act_out, gin_out, mean_out, prec_out, mean_new, prec_new, done
+):
     copies = []
-    for n, (i, k) in enumerate(parts):
-        size = refs[i].shape[0] // (3 if i < 2 else 2)
-        rows = pl.ds(size * k, size)
-        copies.append(pltpu.make_async_copy(refs[i].at[rows], refs[4 + i].at[rows], done.at[n]))
-    for copy in copies:
-        copy.start()
+
+    def send(src, dst, pieces):
+        size = src.shape[0] // pieces
+        for k in range(pieces):
+            rows = pl.ds(size * k, size)
+            copies.append(pltpu.make_async_copy(src.at[rows], dst.at[rows], done.at[len(copies)]))
+            copies[-1].start()
+
+    send(gin, gin_out, 3)
+    send(act, act_out, 3)
+    for t in range(TAPS):
+        rows = pl.ds(16 * t, 16)
+        step = scaled[t].astype(F32)
+        fresh = 0.75 * prec[rows] + 0.25 * step * step
+        prec_new[rows] = fresh
+        mean_new[rows] = mean[rows] - 0.03 * step / (fresh + 0.1)
+    send(prec_new, prec_out, 1)
+    send(mean_new, mean_out, 1)
     for copy in copies:
         copy.wait()
 
@@ -495,16 +505,17 @@
         pltpu.with_memory_space_constraint(v, pltpu.HBM) for v in (feats, og, mean, noise, prec)
     )
     vmem = pl.BlockSpec(memory_space=pltpu.VMEM)
-    act, gin, mean_new, prec_new = pl.pallas_call(
+    *results, scaled = pl.pallas_call(
         functools.partial(kernel, n_dp, n_seg, n_space, near, share),
         out_shape=[
             jax.ShapeDtypeStruct((3, 3, 64, 128), BF16),
             jax.ShapeDtypeStruct((6, 6, 32, 256), BF16),
             jax.ShapeDtypeStruct((TAPS * 16, 128), F32),
             jax.ShapeDtypeStruct((TAPS * 16, 128), F32),
+            jax.ShapeDtypeStruct((TAPS, 16, 128), BF16),
         ],
         in_specs=[pl.BlockSpec(memory_space=pltpu.HBM)] * 5,
-        out_specs=[vmem] * 4,
+        out_specs=[vmem] * 5,
         scratch_shapes=[
             pltpu.VMEM((6, 6, 32, 256), BF16),
             pltpu.VMEM((3, 3, 64, 128), BF16),
@@ -549,12 +560,16 @@
     )(feats, og, mean, noise, prec)
     act, gin, mean_new, prec_new = pl.pallas_call(
         deliver,
-        out_shape=[jax.ShapeDtypeStruct(v.shape, v.dtype) for v in (act, gin, mean_new, prec_new)],
-        in_specs=[vmem] * 4,
+        out_shape=[jax.ShapeDtypeStruct(v.shape, v.dtype) for v in results],
+        in_specs=[vmem] * 5,
         out_specs=[pl.BlockSpec(memory_space=pltpu.HBM)] * 4,
-        scratch_shapes=[pltpu.SemaphoreType.DMA((10,))],
-        compiler_params=pltpu.CompilerParams(vmem_limit_bytes=2**20),
-    )(act, gin, mean_new, prec_new)
+        scratch_shapes=[
+            pltpu.VMEM((TAPS * 16, 128), F32),
+            pltpu.VMEM((TAPS * 16, 128), F32),
+            pltpu.SemaphoreType.DMA((8,)),
+        ],
+        compiler_params=pltpu.CompilerParams(vmem_limit_bytes=4 * 2**20),
+    )(*results, scaled)
     act = jnp.transpose(act, (2, 0, 1, 3))
     gin = jnp.transpose(gin, (2, 0, 1, 3))
     return (

time: 35.7 us -> 35.7 us (level)
  no operation moved by 1% of the time
where the time goes in v6:
time: 35.7 us; the launch traced here: 35.6 us
  Pallas kernels  34.9 us (98%)
  between operations  0.64 us (2%)
    pallas_call x1, Pallas kernels, per_device(): pl.pallas_call(functools.partial(kernel, n_dp, n_seg, n_space, near, shar...  33.9 us
    pallas_call x1, Pallas kernels, per_device(): pl.pallas_call(deliver, out_shape=[jax.ShapeDtypeStruct(v.shape, v.dtype)...  1.07 us

profile of v6, /device:TPU:24, one launch (start us, length us, event | category | flops | bytes accessed | tf_op | source)
XLA Modules:
  0.0 35.6 jit_solution(4616066624743180424)
XLA Ops:
  0.6 33.9 %shard_map.84 = (bf16[3,3,64,128]{3,2,1,0:T(8,128)(2,1)S(1)}, bf16[6,6,32,256]{3,2,1,0:T(8,128)(2,1)S(1)}, f32[432,128]{1,0:T(8,128)S(1)}, f32[432,128]{1,0:T(8,128)S(1)}, bf16[27,16,128]{2,1,0:T(8,128)(2,1)S(1)}) custom-call(bf16[6,6,32,256]{3,2,1,0:T(8,128)(2,1)} %bitcast.17, bf16[3,3,64,128]{3,2,1,0:T(8,128)(2,1)} %bitcast.24, f32[432,128]{1,0:T(8,128)} %bitcast.19, ...), custom_call_target="tpu_custom_call" | custom-call | flops 600000000 | bytes 3000000 | tf_op jit(solution)/shard_map/pallas_call | solution.py:508
  34.5 1.1 %shard_map.85 = (bf16[3,3,64,128]{3,2,1,0:T(8,128)(2,1)}, bf16[6,6,32,256]{3,2,1,0:T(8,128)(2,1)}, f32[432,128]{1,0:T(8,128)}, f32[432,128]{1,0:T(8,128)}) custom-call(bf16[3,3,64,128]{3,2,1,0:T(8,128)(2,1)S(1)} %get-tuple-element.13.act, bf16[6,6,32,256]{3,2,1,0:T(8,128)(2,1)S(1)} %get-tuple-element.14.gin, f32[432,128]{1,0:T(8,128)S(1)} %get-tuple-element.15.mean, ...), custom_call_target="tpu_custom_call" | custom-call | tf_op jit(solution)/shard_map/pallas_call | solution.py:561
